TPU v7x, 32 devices: a whole 2x2x4 slice. The times are simulated.
32 devices in a mesh: section: 4 (over y, x), tok: 8 (over z, core).
Axes of the slice: x: 2, y: 2, z: 4, core: 2. Of those that a mesh axis runs over, the one named last changes fastest.
Arguments:
- stream_one: float32 [4, 512, 1024], P('section', 'tok'), may hold values from -6 to 6
- stream_two: float32 [4, 512, 1024], P('section', 'tok'), may hold values from -6 to 6
- grad_one: bfloat16 [4, 512, 1024], P('section', 'tok'), may hold values from -6 to 6
- grad_two: bfloat16 [4, 512, 1024], P('section', 'tok'), may hold values from -6 to 6
- sensor_ids: int32 [4, 32], P('section'), may hold values from 0 to 7
- block_order: int32 [4, 32], P('section'), may hold values from 0 to 31, each once within a row
- qkv_weight: bfloat16 [4, 1024, 3072], P('section', 'tok'), may hold values from -0.1875 to 0.1875
- out_weight: bfloat16 [4, 1024, 1024], P('section', 'tok'), may hold values from -0.1875 to 0.1875
- attn_gain: float32 [4, 1024], P('section'), may hold values from 0.5 to 1.5
- adapt_gain: float32 [4, 1024], P('section'), may hold values from 0.5 to 1.5
- logit_scale: float32 [4, 8], P('section'), may hold values from 2 to 12
- distance_slope: float32 [4, 8], P('section'), may hold values from 0.02 to 0.6
- adapt_down: bfloat16 [4, 1024, 128], P('section'), may hold values from -0.1875 to 0.1875
- adapt_up: bfloat16 [4, 128, 1024], P('section'), may hold values from -1.5 to 1.5
Outputs:
- inverse_one: float32 [4, 512, 1024], P('section', 'tok')
- inverse_two: float32 [4, 512, 1024], P('section', 'tok')
- cot_one: bfloat16 [4, 512, 1024], P('section', 'tok')
- cot_two: bfloat16 [4, 512, 1024], P('section', 'tok')
- down_grad: bfloat16 [4, 1024, 128], P('section')
- up_grad: bfloat16 [4, 128, 1024], P('section')
Inputs may be any that keep to these rules, and one draw needn't show every extreme that they name: `block_order`: each row names every block place once.
All inputs are finite; a program needn't handle non-finite values.
Results may differ from a plain program's by a relative error of at most 0.02.
Values may be sent and summed in bfloat16 or wider, within the bound.
No kernel may reach another device: no remote copies, remote signals or barrier semaphores. Data moves between devices by JAX's collectives and lax.ppermute only.
A program may use at most 64 MiB of HBM per device.

v0:
```python
import functools

import jax
import jax.numpy as jnp
from jax import lax
from jax.experimental import pallas as pl
from jax.experimental.pallas import tpu as pltpu
from jax.sharding import PartitionSpec as P

RANK = 16
BLOCK = 16
WIN = 32
GROUP = 4
SMALL = 8 * 1024 * 1024
LARGE = 20 * 1024 * 1024
WIDE = 60 * 1024 * 1024

VMEM_SPEC = pl.BlockSpec(memory_space=pltpu.VMEM)
SMEM_SPEC = pl.BlockSpec(memory_space=pltpu.SMEM)
HBM_SPEC = pl.BlockSpec(memory_space=pltpu.HBM)
ANY_SPEC = pl.BlockSpec(memory_space=pl.ANY)


def dot(left, right):
    return jnp.dot(left, right, preferred_element_type=jnp.float32)


def contract_last(left, right):
    return lax.dot_general(
        left, right, (((1,), (1,)), ((), ())), preferred_element_type=jnp.float32
    )


def contract_first(left, right):
    return lax.dot_general(
        left, right, (((0,), (0,)), ((), ())), preferred_element_type=jnp.float32
    )


def normalised(values):
    centred = values - jnp.mean(values, axis=-1, keepdims=True)
    inverse = lax.rsqrt(jnp.mean(centred * centred, axis=-1, keepdims=True) + 1e-05)
    return centred * inverse, inverse


def norm_back(upstream, gain, scaled, inverse):
    inner = upstream * gain
    return inverse * (
        inner
        - jnp.mean(inner, axis=-1, keepdims=True)
        - scaled * jnp.mean(inner * scaled, axis=-1, keepdims=True)
    )


def per_block(ref, row, first, count, shape, dim):
    limit = ref.shape[1] - 1
    place = lax.broadcasted_iota(jnp.int32, shape, dim) // BLOCK
    out = jnp.zeros(shape, jnp.int32)
    for k in range(count):
        out = jnp.where(place == k, ref[row, jnp.clip(first + k, 0, limit)], out)
    return out


def adapter_kernel(packed, *refs):
    refs = list(refs)
    blocks_ref = refs.pop(0)
    if packed:
        late_ref, early_ref = refs.pop(0), refs.pop(0)
        rows = late_ref.shape[0] // 2
        top, bottom_cot = late_ref[:rows], late_ref[rows:]
        bottom, top_cot = early_ref[:rows], early_ref[rows:]
    else:
        top, bottom, top_cot, bottom_cot = [refs.pop(0)[...] for _ in range(4)]
        rows = top.shape[0]
    gain_a_ref, gain_f_ref, down_ref, up_ref = refs[:4]
    bottom_ref_out, z_ref, up_msg_ref, down_msg_ref, own_ref = refs[4:9]
    next_ref, na_ref, dhid_ref, hid_ref = refs[9:]
    columns = down_ref.shape[1]
    first = lax.axis_index("tok") * (rows // BLOCK)
    shape = (rows, columns)
    owner = lax.broadcasted_iota(jnp.int32, shape, 1) // RANK
    sensor = per_block(blocks_ref, 0, first, rows // BLOCK, shape, 0)
    mask = (owner == sensor).astype(jnp.float32)
    gain_a = gain_a_ref[...]
    scaled, inverse = normalised(top.astype(jnp.float32))
    na = (scaled * gain_a).astype(jnp.bfloat16)
    pre = mask * dot(na, down_ref[...])
    phi = 0.5 * (1.0 + lax.erf(pre * 0.7071067811865476))
    hid = (pre * phi).astype(jnp.bfloat16)
    bottom = bottom.astype(jnp.float32) - dot(hid, up_ref[...])
    slope = phi + pre * jnp.exp(-0.5 * pre * pre) * 0.3989422804014327
    dhid = (mask * slope * contract_last(bottom_cot, up_ref[...])).astype(jnp.bfloat16)
    dna = contract_last(dhid, down_ref[...])
    z = top_cot.astype(jnp.float32) + norm_back(dna, gain_a, scaled, inverse)
    z = z.astype(jnp.bfloat16)
    nf = (normalised(bottom)[0] * gain_f_ref[...]).astype(jnp.bfloat16)
    bottom_ref_out[...] = bottom
    z_ref[...] = z
    own_ref[:rows] = nf
    own_ref[rows:] = z
    up_msg_ref[:rows] = nf
    up_msg_ref[rows:] = z[rows - WIN :]
    down_msg_ref[:rows] = nf
    down_msg_ref[rows:] = z[:WIN]
    next_ref[:rows] = bottom.astype(jnp.bfloat16)
    next_ref[rows:] = z
    na_ref[...] = na
    dhid_ref[...] = dhid
    hid_ref[...] = hid


def adapter(packed, blocks, streams, gain_a, gain_f, down, up):
    width, columns = down.shape
    rows = streams[0].shape[0] // (2 if packed else 1)
    bf = jnp.bfloat16
    shape = jax.ShapeDtypeStruct
    outs = (
        shape((rows, width), jnp.float32),
        shape((rows, width), bf),
        shape((rows + WIN, width), bf),
        shape((rows + WIN, width), bf),
        shape((2 * rows, width), bf),
        shape((2 * rows, width), bf),
        shape((rows, width), bf),
        shape((rows, columns), bf),
        shape((rows, columns), bf),
    )
    return pl.pallas_call(
        functools.partial(adapter_kernel, packed),
        out_shape=outs,
        in_specs=[SMEM_SPEC] + [VMEM_SPEC] * (len(streams) + 4),
        out_specs=(VMEM_SPEC,) * len(outs),
        compiler_params=pltpu.CompilerParams(vmem_limit_bytes=SMALL),
        cost_estimate=pl.CostEstimate(
            flops=8 * rows * width * columns, bytes_accessed=20 * rows * width, transcendentals=0
        ),
        name="adapter",
    )(blocks, *streams, gain_a, gain_f, down, up)


def grads_kernel(
    na_a, na_b, dhid_a, dhid_b, hid_a, hid_b, cot_a, late_ref, keep_ref, send_ref, both
):
    rows, columns = dhid_a.shape
    core = lax.rem(lax.axis_index("tok"), 2)
    cot_b = late_ref[rows:]
    both[0] = contract_first(dhid_a[...], na_a[...]) + contract_first(dhid_b[...], na_b[...])
    both[1] = contract_first(hid_a[...], cot_a[...]) + contract_first(hid_b[...], cot_b)
    keep_ref[...] = both[core]
    send_ref[...] = both[1 - core].astype(jnp.bfloat16)


def adapter_grads(*arrays):
    rows, width = arrays[0].shape
    columns = arrays[2].shape[1]
    return pl.pallas_call(
        grads_kernel,
        out_shape=(
            jax.ShapeDtypeStruct((columns, width), jnp.float32),
            jax.ShapeDtypeStruct((columns, width), jnp.bfloat16),
        ),
        in_specs=[VMEM_SPEC] * 8,
        out_specs=(VMEM_SPEC,) * 2,
        scratch_shapes=[pltpu.VMEM((2, columns, width), jnp.float32)],
        compiler_params=pltpu.CompilerParams(vmem_limit_bytes=SMALL),
        cost_estimate=pl.CostEstimate(
            flops=8 * rows * width * columns, bytes_accessed=10 * rows * width, transcendentals=0
        ),
        name="adapter_grads",
    )(*arrays)


def core_sum_kernel(keep_ref, came_ref, out_ref, *send_refs):
    parts, depth, _ = out_ref.shape
    chip = lax.axis_index("tok") // 2
    for i in range(parts):
        at = slice(i * depth, (i + 1) * depth)
        total = keep_ref[at] + came_ref[at].astype(jnp.float32)
        out_ref[i] = total.astype(jnp.bfloat16)
    for hops, send_ref in enumerate(send_refs, 1):
        send_ref[...] = out_ref[lax.rem(chip + hops, parts)]


def core_sum(keep, came, parts):
    columns, width = keep.shape
    return pl.pallas_call(
        core_sum_kernel,
        out_shape=(jax.ShapeDtypeStruct((parts, columns // parts, width), jnp.bfloat16),)
        + (jax.ShapeDtypeStruct((columns // parts, width), jnp.bfloat16),) * (parts - 1),
        in_specs=[VMEM_SPEC] * 2,
        out_specs=(VMEM_SPEC,) * parts,
        compiler_params=pltpu.CompilerParams(vmem_limit_bytes=SMALL),
        name="core_sum",
    )(keep, came)


def chip_sum_kernel(parts_ref, *refs):
    after_ref, out_ref = refs[-2:]
    del after_ref
    chips = parts_ref.shape[0]
    chip = lax.axis_index("tok") // 2
    total = parts_ref[chip].astype(jnp.float32)
    for came_ref in refs[: chips - 1]:
        total += came_ref[...].astype(jnp.float32)
    out_ref[...] = total.astype(jnp.bfloat16)


def chip_sum(parts, came, after):
    return pl.pallas_call(
        chip_sum_kernel,
        out_shape=jax.ShapeDtypeStruct(parts.shape[1:], parts.dtype),
        in_specs=[VMEM_SPEC] * (1 + len(came)) + [ANY_SPEC],
        out_specs=VMEM_SPEC,
        compiler_params=pltpu.CompilerParams(vmem_limit_bytes=SMALL),
        name="chip_sum",
    )(parts, *came, after)


def join_kernel(*refs):
    *block_refs, after_ref, out_ref = refs
    del after_ref
    chips, depth = len(block_refs), block_refs[0].shape[0]
    chip = lax.axis_index("tok") // 2
    for hops, block_ref in enumerate(block_refs):
        row = lax.rem(chip - hops + chips, chips) * depth
        out_ref[pl.ds(pl.multiple_of(row, depth), depth)] = block_ref[...]


def joined(blocks, after):
    depth, width = blocks[0].shape
    return pl.pallas_call(
        join_kernel,
        out_shape=jax.ShapeDtypeStruct((len(blocks) * depth, width), blocks[0].dtype),
        in_specs=[VMEM_SPEC] * len(blocks) + [ANY_SPEC],
        out_specs=VMEM_SPEC,
        compiler_params=pltpu.CompilerParams(vmem_limit_bytes=SMALL),
        name="joined",
    )(*blocks, after)


def finish_kernel(mine_ref, other_ref, down_ref, up_ref):
    core = lax.rem(lax.axis_index("tok"), 2)

    def write(down, up):
        down_ref[...] = down[...].astype(jnp.float32).T.astype(jnp.bfloat16)
        up_ref[...] = up[...]

    pl.when(core == 0)(lambda: write(mine_ref, other_ref))
    pl.when(core != 0)(lambda: write(other_ref, mine_ref))


def finish(mine, other):
    columns, width = mine.shape
    return pl.pallas_call(
        finish_kernel,
        out_shape=(
            jax.ShapeDtypeStruct((width, columns), mine.dtype),
            jax.ShapeDtypeStruct((columns, width), mine.dtype),
        ),
        in_specs=[VMEM_SPEC] * 2,
        out_specs=(VMEM_SPEC,) * 2,
        compiler_params=pltpu.CompilerParams(vmem_limit_bytes=SMALL),
        name="finish",
    )(mine, other)


def arrange_kernel(sizes, pair, weight_hbm, out_weight_hbm, *refs):
    whole_ref, *part_refs, weight_ref, out_weight_ref, sems = refs
    copies = [
        pltpu.make_async_copy(weight_hbm, weight_ref, sems.at[0]),
        pltpu.make_async_copy(out_weight_hbm, out_weight_ref, sems.at[1]),
    ]
    for copy in copies:
        copy.start()
    for copy in copies:
        copy.wait()
    width = weight_ref.shape[1] // 3
    at = first = 0
    for part, pairs in enumerate(sizes):
        begin = at
        for j in range(first, first + pairs):
            for kind in range(3):
                column = kind * width + j * pair
                whole_ref[:, at : at + pair] = weight_ref[:, column : column + pair]
                at += pair
        first += pairs
        if part == 0:
            whole_ref[:, at : at + width] = out_weight_ref[...]
            at += width
        part_refs[part][...] = whole_ref[:, begin:at]


def arrange(weight, out_weight, sizes, pair):
    depth, width = out_weight.shape
    columns = [3 * pair * pairs + (width if part == 0 else 0) for part, pairs in enumerate(sizes)]
    return pl.pallas_call(
        functools.partial(arrange_kernel, sizes, pair),
        out_shape=tuple(
            jax.ShapeDtypeStruct((depth, size), weight.dtype) for size in [sum(columns)] + columns
        ),
        in_specs=[HBM_SPEC] * 2,
        out_specs=(VMEM_SPEC,) * 3,
        scratch_shapes=[
            pltpu.VMEM(weight.shape, weight.dtype),
            pltpu.VMEM(out_weight.shape, out_weight.dtype),
            pltpu.SemaphoreType.DMA((2,)),
        ],
        compiler_params=pltpu.CompilerParams(vmem_limit_bytes=WIDE),
        name="arrange",
    )(weight, out_weight)


def part_kernel(begin, values_ref, *refs):
    out_ref = refs[-1]
    out_ref[...] = values_ref[:, begin : begin + out_ref.shape[1]]


def part_of(values, begin, size, *after):
    return pl.pallas_call(
        functools.partial(part_kernel, begin),
        out_shape=jax.ShapeDtypeStruct((values.shape[0], size), values.dtype),
        in_specs=[VMEM_SPEC] + [ANY_SPEC] * len(after),
        out_specs=VMEM_SPEC,
        compiler_params=pltpu.CompilerParams(vmem_limit_bytes=SMALL),
        name="part_of",
    )(values, *after)


def gate_kernel(*refs):
    del refs


def gate(values, *after):
    return pl.pallas_call(
        gate_kernel,
        out_shape=jax.ShapeDtypeStruct(values.shape, values.dtype),
        in_specs=[ANY_SPEC] * (1 + len(after)),
        out_specs=ANY_SPEC,
        input_output_aliases={0: 0},
        compiler_params=pltpu.CompilerParams(vmem_limit_bytes=SMALL),
        name="gate",
    )(values, *after)


def order_kernel(begins, *refs):
    *shard_refs, out_ref = refs
    shards, depth = len(shard_refs), shard_refs[0].shape[0]
    columns = out_ref.shape[1]
    me = lax.axis_index("tok")
    chip, core = me // 2, lax.rem(me, 2)
    for i, (begin, shard_ref) in enumerate(zip(begins, shard_refs)):
        hops, other = divmod(i, 2)
        chip_from = lax.rem(chip - hops + shards // 2, shards // 2)
        row = (2 * chip_from + (1 - core if other else core)) * depth
        at = pl.ds(pl.multiple_of(row, depth), depth)
        out_ref[at] = shard_ref[:, begin : begin + columns]


def ordered(shards, begins, columns):
    depth = shards[0].shape[0]
    return pl.pallas_call(
        functools.partial(order_kernel, tuple(begins)),
        out_shape=jax.ShapeDtypeStruct((len(shards) * depth, columns), shards[0].dtype),
        in_specs=[VMEM_SPEC] * len(shards),
        out_specs=VMEM_SPEC,
        compiler_params=pltpu.CompilerParams(vmem_limit_bytes=SMALL),
        name="ordered",
    )(*shards)


def attention_kernel(pairs, first_pair, is_first, ends, waits, *refs):
    refs = list(refs)
    take = lambda count: [refs.pop(0) for _ in range(count)]
    order_ref, scale_ref, slope_ref, own_ref, before_ref, after_ref, w_ref, wo_ref = take(8)
    partial_refs = [] if is_first else take(2)
    if ends == "one":
        top_ref, bottom_ref, bottom_cot_ref, gain_ref = take(4)
        take(waits)
        (send_ref,) = take(1)
    elif ends == "two":
        late_ref, bottom_ref, gain_ref = take(3)
        take(waits)
        top_out_ref, cot_out_ref, done_ref = take(3)
    else:
        take(waits)
        top_part_ref, nf_part_ref, done_ref = take(3)
    nf_all, z_all, logs, top_acc, nf_acc = refs

    rows, width = top_acc.shape
    head_size = width // scale_ref.shape[1]
    pair = GROUP * head_size
    wide = 3 * pair
    queries, keys = rows + 2 * WIN, 3 * rows
    nf_all[:rows] = own_ref[:rows]
    nf_all[rows : 2 * rows] = after_ref[:rows]
    nf_all[2 * rows :] = before_ref[:rows]
    z_all[:rows] = own_ref[rows:]
    z_all[rows : rows + WIN] = after_ref[rows:]
    z_all[rows + WIN :] = before_ref[rows:]
    if is_first:
        top_acc[...] = jnp.zeros_like(top_acc)
        nf_acc[...] = jnp.zeros_like(nf_acc)
    else:
        top_acc[...] = partial_refs[0][...]
        nf_acc[...] = partial_refs[1][...]
    total = order_ref.shape[1] * BLOCK
    start = lax.axis_index("tok") * rows
    first = lax.axis_index("tok") * (rows // BLOCK)
    here = rows // BLOCK
    reach = WIN // BLOCK

    def places(shape, dim, lead, tail):
        at = lax.broadcasted_iota(jnp.int32, shape, dim)
        own_and_after = per_block(order_ref, 1, first, here + lead, shape, dim)
        skip = here + lead
        ahead = per_block(order_ref, 1, first - tail - skip, skip + tail, shape, dim)
        is_before = at >= rows + lead * BLOCK
        place = jnp.where(is_before, ahead, own_and_after)
        token = jnp.where(is_before, at - rows - (lead + tail) * BLOCK, at) + start
        return place, token

    query_place, query_token = places((queries, 1), 0, reach, reach)
    key_place, key_token = places((1, keys), 1, here, here)
    near = jnp.abs(query_token - key_token) <= WIN
    allowed = near & (key_token >= 0) & (key_token < total)
    gap = jnp.abs(query_place - key_place).astype(jnp.float32)
    logs[...] = jnp.where(allowed, jnp.log(1.0 + gap), -1.0)


    for step in range(pairs):
        nf = nf_all[...]
        nf_queries = jnp.concatenate([nf[: rows + WIN], nf[3 * rows - WIN :]], axis=0)
        columns = lambda part: pl.ds((3 * step + part) * pair, pair)
        w_now = w_ref.at[:, pl.ds(step * wide, wide)]
        wo_now = wo_ref.at[
            pl.ds((first_pair + step) * pair, pair),
            wo_ref.shape[1] - width :,
        ]
        q_all = dot(nf_queries, w_ref[:, columns(0)])
        k_all = dot(nf, w_ref[:, columns(1)])
        v_all = dot(nf, w_ref[:, columns(2)])
        dob_all = contract_last(z_all[...], wo_now[...]).astype(jnp.bfloat16)
        logs_now = logs[...]
        mixed, dq_all, dk_all, dv_all = [], [], [], []
        for local in range(pair // head_size):
            head = (first_pair + step) * (pair // head_size) + local
            part = slice(local * head_size, (local + 1) * head_size)
            factor = scale_ref[0, head] * (1.0 / head_size)
            q, k, vb, dob = q_all[:, part], k_all[:, part], v_all[:, part], dob_all[:, part]
            vb = vb.astype(jnp.bfloat16)
            q_inv = lax.rsqrt(jnp.mean(q * q, axis=-1, keepdims=True) + 1e-06)
            k_inv = lax.rsqrt(jnp.mean(k * k, axis=-1, keepdims=True) + 1e-06)
            qn, kn = q * q_inv, k * k_inv
            qb, kb = qn.astype(jnp.bfloat16), kn.astype(jnp.bfloat16)
            score = contract_last(qb, kb) * factor - slope_ref[0, head] * logs_now
            weights = jnp.where(logs_now >= 0.0, jnp.exp(score), 0.0)
            prob = weights / jnp.sum(weights, axis=-1, keepdims=True)
            prob_bf = prob.astype(jnp.bfloat16)
            mixed.append(dot(prob_bf[:rows], vb).astype(jnp.bfloat16))
            dprob = contract_last(dob, vb)
            centre = jnp.sum(prob * dprob, axis=-1, keepdims=True)
            dscore = (prob * (dprob - centre) * factor).astype(jnp.bfloat16)
            dqn = dot(dscore[:rows], kb)
            dkn = contract_first(dscore[:, : 2 * rows], qb)[:rows]
            dv = contract_first(prob_bf[:, : 2 * rows], dob)[:rows]
            qn, kn, q_inv, k_inv = qn[:rows], kn[:rows], q_inv[:rows], k_inv[:rows]
            dq = q_inv * (dqn - qn * jnp.mean(dqn * qn, axis=-1, keepdims=True))
            dk = k_inv * (dkn - kn * jnp.mean(dkn * kn, axis=-1, keepdims=True))
            dq_all.append(dq.astype(jnp.bfloat16))
            dk_all.append(dk.astype(jnp.bfloat16))
            dv_all.append(dv.astype(jnp.bfloat16))
        top_acc[...] += dot(jnp.concatenate(mixed, axis=1), wo_now[...])
        nf_acc[...] += contract_last(jnp.concatenate(dq_all + dk_all + dv_all, axis=1), w_now[...])

    if ends != "one":
        done_ref[...] = jnp.zeros_like(done_ref)
    if ends is None:
        top_part_ref[...] = top_acc[...]
        nf_part_ref[...] = nf_acc[...]
        return
    if ends == "one":
        top, bottom_cot = top_ref[...], bottom_cot_ref[...]
    else:
        top, bottom_cot = late_ref[:rows], late_ref[rows:]
    top = top.astype(jnp.float32) - top_acc[...]
    scaled, inverse = normalised(bottom_ref[...])
    back = norm_back(nf_acc[...], gain_ref[...], scaled, inverse)
    cot = (bottom_cot.astype(jnp.float32) + back).astype(jnp.bfloat16)
    if ends == "one":
        send_ref[:rows] = top.astype(jnp.bfloat16)
        send_ref[rows:] = cot
    else:
        top_out_ref[...] = top
        cot_out_ref[...] = cot


def attention(blocks, weight, out_weight, first_pair, pairs, partial, ends, last, after):
    order, scale, slope, own, before, behind = blocks
    rows, width = own.shape[0] // 2, own.shape[1]
    bf = jnp.bfloat16
    arrays = list(blocks) + [weight, out_weight] + list(partial or ()) + list(last)
    own_rows = jax.ShapeDtypeStruct((rows, width), jnp.float32)
    if ends == "one":
        outs = (jax.ShapeDtypeStruct((2 * rows, width), bf),)
    elif ends == "two":
        outs = (own_rows, jax.ShapeDtypeStruct((rows, width), bf))
    else:
        outs = (own_rows, own_rows)
    if ends != "one":
        outs += (jax.ShapeDtypeStruct((8, 128), jnp.float32),)
    return pl.pallas_call(
        functools.partial(
            attention_kernel, pairs, first_pair, partial is None, ends, len(after)
        ),
        out_shape=outs,
        in_specs=[SMEM_SPEC] * 3 + [VMEM_SPEC] * (len(arrays) - 3) + [ANY_SPEC] * len(after),
        out_specs=(VMEM_SPEC,) * len(outs),
        scratch_shapes=[
            pltpu.VMEM((3 * rows, width), bf),
            pltpu.VMEM((rows + 2 * WIN, width), bf),
            pltpu.VMEM((rows + 2 * WIN, 3 * rows), jnp.float32),
            pltpu.VMEM((rows, width), jnp.float32),
            pltpu.VMEM((rows, width), jnp.float32),
        ],
        compiler_params=pltpu.CompilerParams(vmem_limit_bytes=LARGE),
        cost_estimate=pl.CostEstimate(
            flops=8 * pairs * rows * width * width,
            bytes_accessed=2 * pairs * width * width,
            transcendentals=0,
        ),
        name="attention",
    )(*arrays, *after)


def shifted(values, axis, by):
    devices = lax.axis_size(axis)
    pairs = [(i, i + by) for i in range(devices) if 0 <= i + by < devices]
    return lax.ppermute(values, axis, pairs)


def rotated(values, hops=1):
    devices = lax.axis_size("tok")
    pairs = [(i, (i + 2 * hops) % devices) for i in range(devices)]
    return lax.ppermute(values, "tok", pairs)


def swapped(values):
    devices = lax.axis_size("tok")
    return lax.ppermute(values, "tok", [(i, i ^ 1) for i in range(devices)])


def on_device(
    stream_one, stream_two, grad_one, grad_two, sensor_ids, block_order, qkv_weight, out_weight,
    attn_gain, adapt_gain, logit_scale, distance_slope, adapt_down, adapt_up,
):
    chips = lax.axis_size("tok") // 2
    width = adapt_up.shape[2]
    heads = logit_scale.shape[1]
    groups = heads // GROUP
    pair = GROUP * (width // heads)
    half = groups // 2
    params = (adapt_gain, attn_gain, adapt_down[0], adapt_up[0])

    blocks = jnp.concatenate([sensor_ids, block_order], axis=0)
    next_blocks = shifted(blocks, "section", -1)
    streams = (stream_one[0], stream_two[0], grad_one[0], grad_two[0])
    one = adapter(False, blocks, streams, *params)
    bottom_one, _, up_msg, down_msg, own, next_early, na_one, dhid_one, hid_one = one
    before, behind = shifted(up_msg, "tok", 1), shifted(down_msg, "tok", -1)
    early = shifted(next_early, "section", -1)

    whole, x_own, y_own = arrange(qkv_weight[0], out_weight[0], (half, groups - half), pair)
    x_size, y_size = x_own.shape[1], y_own.shape[1]
    ups = chips // 2
    up_whole = rotated(whole)
    whole_other = swapped(part_of(whole, 0, whole.shape[1], before, behind))
    x_up, y_up = [], []
    if ups > 1:
        x_up.append(rotated(part_of(up_whole, 0, x_size, own)))
        y_up.append(rotated(part_of(up_whole, x_size, y_size, own, own)))
    x_down, y_down = [x_own], [y_own]
    for _ in range(chips - 1 - ups):
        x_down.append(rotated(x_down[-1], -1))
        y_down.append(rotated(y_down[-1], -1))
    for _ in range(ups - 2):
        x_up.append(rotated(x_up[-1]))
        y_up.append(rotated(y_up[-1]))

    up_other = swapped(part_of(up_whole, 0, whole.shape[1], y_down[-1]))
    both_whole = [whole, whole_other, up_whole, up_other]

    def gathered(rest, begin, size):
        shards = both_whole + [shard for mine in rest for shard in (mine, swapped(mine))]
        return ordered(shards, [begin] * 4 + [0] * (2 * len(rest)), size)

    w_x = gathered(x_up + x_down[:0:-1], 0, x_size)
    head_args = (blocks, logit_scale, distance_slope, own, before, behind)
    *part, done = attention(
        head_args, w_x, w_x, 0, half, None, None, (), (y_down[-1],)
    )
    y_up[-1] = gate(y_up[-1], done, early, next_blocks)
    w_y = gathered(y_up + y_down[:0:-1], x_size, y_size)
    last = (stream_one[0], bottom_one, grad_two[0], attn_gain)
    (late,) = attention(head_args, w_y, w_x, half, groups - half, part, "one", last, ())
    late = shifted(late, "section", -1)

    two = adapter(True, next_blocks, (late, early), *params)
    bottom_two, z_two, up_msg, down_msg, own, _, na_two, dhid_two, hid_two = two
    before, behind = shifted(up_msg, "tok", 1), shifted(down_msg, "tok", -1)
    keep, send = adapter_grads(
        na_one, na_two, dhid_one, dhid_two, hid_one, hid_two, grad_two[0], late
    )
    parts, *sends = core_sum(keep, swapped(send), chips)
    came = [rotated(block, hops) for hops, block in enumerate(sends, 1)]
    head_args = (next_blocks, logit_scale, distance_slope, own, before, behind)
    *part, done = attention(head_args, w_x, w_x, 0, half, None, None, (), (parts,))
    block = chip_sum(parts, came, done)
    blocks_all = [block] + [rotated(block, hops) for hops in range(1, chips)]
    top_two, cot_two, done = attention(
        head_args, w_y, w_x, half, groups - half, part, "two", (late, bottom_two, attn_gain),
        (block,),
    )
    mine = joined(blocks_all, done)
    down_grad, up_grad = finish(mine, swapped(mine))
    return (
        top_two[None],
        bottom_two[None],
        z_two[None],
        cot_two[None],
        down_grad[None],
        up_grad[None],
    )


def solution(mesh):
    tokens = P("section", "tok", None)
    section = P("section", None)
    whole = P("section", None, None)
    return jax.shard_map(
        on_device,
        mesh=mesh,
        in_specs=(tokens,) * 4
        + (section,) * 2
        + (tokens,) * 2
        + (section,) * 4
        + (whole,) * 2,
        out_specs=(tokens,) * 4 + (whole,) * 2,
        check_vma=False,
    )
```

profile of v0, /device:TPU:0, one launch (start us, length us, event | category | flops | bytes accessed | tf_op | source)
XLA Modules:
  0.0 129.5 jit_solution(11800415700330610553)
XLA Ops:
  0.6 2.6 %arrange.1 = (bf16[128,4096]{1,0:T(8,128)(2,1)}, bf16[128,2560]{1,0:T(8,128)(2,1)}, bf16[128,1536]{1,0:T(8,128)(2,1)}) custom-call(bf16[128,3072]{1,0:T(8,128)(2,1)} %bitcast.26, bf16[128,1024]{1,0:T(8,128)(2,1)} %bitcast.27), custom_call_target="tpu_custom_call" | custom-call | tf_op jit(solution)/shard_map/arrange/pallas_call | solution.py:296
  3.3 3.1 %collective-permute-start.4 = (bf16[128,4096]{1,0:T(8,128)(2,1)}, bf16[128,4096]{1,0:T(8,128)(2,1)S(1)}, u32[]{:S(2)}, u32[]{:S(2)}) collective-permute-start(bf16[128,4096]{1,0:T(8,128)(2,1)} %get-tuple-element.45.values_ref.refs_0_), channel_id=1, source_target_pairs={{0,2},{1,3},{2,4},{3,5},{4,6},{5,7},{6,0},{7,1},{8,10},{9,11},{10,... | collective-permute-start | bytes 3145736 | tf_op jit(solution)/shard_map/ppermute | solution.py:544
  14.0 2.2 %adapter.2 = (f32[64,1024]{1,0:T(8,128)S(1)}, bf16[64,1024]{1,0:T(8,128)(2,1)}, bf16[96,1024]{1,0:T(8,128)(2,1)S(1)}, bf16[96,1024]{1,0:T(8,128)(2,1)S(1)}, bf16...) custom-call(s32[2,32]{1,0:T(2,128)S(1)} %pad_add_fusion.refs_0_, ...), custom_call_target="tpu_custom_call" | custom-call | flops 67108864 | bytes 1310720 | tf_op jit(solution)/shard_map/adapter/pallas_call | solution.py:128
  19.0 5.0 %collective-permute-start.5 = (bf16[128,1536]{1,0:T(8,128)(2,1)}, bf16[128,1536]{1,0:T(8,128)(2,1)S(1)}, u32[]{:S(2)}, u32[]{:S(2)}) collective-permute-start(bf16[128,1536]{1,0:T(8,128)(2,1)} %get-tuple-element.46), channel_id=1, source_target_pairs={{0,6},{1,7},{2,0},{3,1},{4,2},{5,3},{6,4},{7,5},{8,14},{9,15},{10,... | collective-permute-start | bytes 1179656 | tf_op jit(solution)/shard_map/ppermute | solution.py:544
  24.0 1.9 %collective-permute-start.10 = (bf16[128,2560]{1,0:T(8,128)(2,1)}, bf16[128,2560]{1,0:T(8,128)(2,1)S(1)}, u32[]{:S(2)}, u32[]{:S(2)}) collective-permute-start(bf16[128,2560]{1,0:T(8,128)(2,1)} %get-tuple-element.47), channel_id=1, source_target_pairs={{0,6},{1,7},{2,0},{3,1},{4,2},{5,3},{6,4},{7,5},{8,14},{9,15},{10,... | collective-permute-start | bytes 1966088 | tf_op jit(solution)/shard_map/ppermute | solution.py:544
  25.9 6.7 %collective-permute-done.4.values_ref.refs_2_ = bf16[128,4096]{1,0:T(8,128)(2,1)S(1)} collective-permute-done((bf16[128,4096]{1,0:T(8,128)(2,1)}, bf16[128,4096]{1,0:T(8,128)(2,1)S(1)}, u32[]{:S(2)}, u32[]{:S(2)}) %collective-permute-start.4) | collective-permute-done | bytes 1048608 | tf_op jit(solution)/shard_map/ppermute | solution.py:544
  34.0 3.1 %collective-permute-start.3 = (bf16[128,4096]{1,0:T(8,128)(2,1)S(1)}, bf16[128,4096]{1,0:T(8,128)(2,1)S(1)}, u32[]{:S(2)}, u32[]{:S(2)}) collective-permute-start(bf16[128,4096]{1,0:T(8,128)(2,1)S(1)} %part_of.4), channel_id=1, source_target_pairs={{0,1},{1,0},{2,3},{3,2},{4,5},{5,4},{6,7},{7,6},{8,9},{9,8},{10,11... | collective-permute-start | bytes 3145736 | tf_op jit(solution)/shard_map/ppermute | solution.py:549
  37.1 7.2 %collective-permute-done.5.refs_0_.refs_8_.refs_6_ = bf16[128,1536]{1,0:T(8,128)(2,1)S(1)} collective-permute-done((bf16[128,1536]{1,0:T(8,128)(2,1)}, bf16[128,1536]{1,0:T(8,128)(2,1)S(1)}, u32[]{:S(2)}, u32[]{:S(2)}) %collective-permute-start.5) | collective-permute-done | bytes 393248 | tf_op jit(solution)/shard_map/ppermute | solution.py:544
  44.5 14.7 %collective-permute-done.10.refs_6_ = bf16[128,2560]{1,0:T(8,128)(2,1)S(1)} collective-permute-done((bf16[128,2560]{1,0:T(8,128)(2,1)}, bf16[128,2560]{1,0:T(8,128)(2,1)S(1)}, u32[]{:S(2)}, u32[]{:S(2)}) %collective-permute-start.10) | collective-permute-done | bytes 655392 | tf_op jit(solution)/shard_map/ppermute | solution.py:544
  59.2 11.2 %collective-permute-done.8.refs_4_ = bf16[128,2560]{1,0:T(8,128)(2,1)S(1)} collective-permute-done((bf16[128,2560]{1,0:T(8,128)(2,1)S(1)}, bf16[128,2560]{1,0:T(8,128)(2,1)S(1)}, u32[]{:S(2)}, u32[]{:S(2)}) %collective-permute-start.8) | collective-permute-done | bytes 655392 | tf_op jit(solution)/shard_map/ppermute | solution.py:544
  74.1 3.9 %attention.4 = (f32[64,1024]{1,0:T(8,128)S(1)}, f32[64,1024]{1,0:T(8,128)S(1)}, f32[8,128]{1,0:T(8,128)S(1)}) custom-call(s32[2,32]{1,0:T(2,128)S(1)} %pad_add_fusion.refs_0_, f32[1,8]{1,0:T(1,128)S(1)} %copy-done.17, f32[1,8]{1,0:T(1,128)S(1)} %copy-done.18, bf16[128,1024]{1,0:T(8,128)(2,1)S(1)} %get-tuple-element.42.refs_0_.refs_1_.refs_3_, ...), custom_call_target="tpu_custom_call" | custom-call | flops 536870912 | bytes 2097152 | tf_op jit(solution)/shard_map/attention/pallas_call | solution.py:511
  78.1 3.1 %collective-permute-done.refs_3_.refs_0_ = s32[2,32]{1,0:T(2,128)S(1)} collective-permute-done((s32[2,32]{1,0:T(2,128)S(1)}, s32[2,32]{1,0:T(2,128)S(1)}, u32[]{:S(2)}, u32[]{:S(2)}) %collective-permute-start) | collective-permute-done | bytes 288 | tf_op jit(solution)/shard_map/ppermute | solution.py:538
  81.2 2.6 %collective-permute-done.7.refs_0_ = bf16[128,1536]{1,0:T(8,128)(2,1)S(1)} collective-permute-done((bf16[128,1536]{1,0:T(8,128)(2,1)S(1)}, bf16[128,1536]{1,0:T(8,128)(2,1)S(1)}, u32[]{:S(2)}, u32[]{:S(2)}) %collective-permute-start.7) | collective-permute-done | bytes 393248 | tf_op jit(solution)/shard_map/ppermute | solution.py:544
  83.8 1.7 %collective-permute-done.13.refs_5_ = bf16[128,1536]{1,0:T(8,128)(2,1)S(1)} collective-permute-done((bf16[128,1536]{1,0:T(8,128)(2,1)S(1)}, bf16[128,1536]{1,0:T(8,128)(2,1)S(1)}, u32[]{:S(2)}, u32[]{:S(2)}) %collective-permute-start.13) | collective-permute-done | bytes 393248 | tf_op jit(solution)/shard_map/ppermute | solution.py:549
  85.8 4.0 %attention.5 = bf16[128,1024]{1,0:T(8,128)(2,1)S(1)} custom-call(s32[2,32]{1,0:T(2,128)S(1)} %pad_add_fusion.refs_0_, f32[1,8]{1,0:T(1,128)S(1)} %copy-done.17, f32[1,8]{1,0:T(1,128)S(1)} %copy-done.18, bf16[128,1024]{1,0:T(8,128)(2,1)S(1)} %get-tuple-element.42.refs_0_.refs_1_.refs_3_, bf16[96,1024]{1,0:T(8,128)(2,1)S(1)} %collective-permute-done.1.refs_0_.refs_4_, ...), custom_call_target="tpu_custom_call" | custom-call | flops 536870912 | bytes 2097152 | tf_op jit(solution)/shard_map/attention/pallas_call | solution.py:511
  91.2 8.9 %collective-permute-done.15.refs_1_.late_ref.refs_10_ = bf16[128,1024]{1,0:T(8,128)(2,1)S(1)} collective-permute-done((bf16[128,1024]{1,0:T(8,128)(2,1)S(1)}, bf16[128,1024]{1,0:T(8,128)(2,1)S(1)}, u32[]{:S(2)}, u32[]{:S(2)}) %collective-permute-start.15) | collective-permute-done | bytes 262176 | tf_op jit(solution)/shard_map/ppermute | solution.py:538
  100.1 2.3 %adapter.3 = (f32[64,1024]{1,0:T(8,128)}, bf16[64,1024]{1,0:T(8,128)(2,1)}, bf16[96,1024]{1,0:T(8,128)(2,1)S(1)}, bf16[96,1024]{1,0:T(8,128)(2,1)S(1)}, bf16[128...) custom-call(s32[2,32]{1,0:T(2,128)S(1)} %collective-permute-done.ref, ...), custom_call_target="tpu_custom_call" | custom-call | flops 67108864 | bytes 1310720 | tf_op jit(solution)/shard_map/adapter/pallas_call | solution.py:128
  103.1 2.4 %collective-permute-start.16 = (bf16[96,1024]{1,0:T(8,128)(2,1)S(1)}, bf16[96,1024]{1,0:T(8,128)(2,1)S(1)}, u32[]{:S(2)}, u32[]{:S(2)}) collective-permute-start(bf16[96,1024]{1,0:T(8,128)(2,1)S(1)} %get-tuple-element.54), channel_id=1, source_target_pairs={{0,1},{1,2},{2,3},{3,4},{4,5},{5,6},{6,7},{8,9},{9,10},{10,11},{11... | collective-permute-start | bytes 589832 | tf_op jit(solution)/shard_map/ppermute | solution.py:538
  106.9 2.3 %collective-permute-start.19 = (bf16[32,1024]{1,0:T(8,128)(2,1)S(1)}, bf16[32,1024]{1,0:T(8,128)(2,1)S(1)}, u32[]{:S(2)}, u32[]{:S(2)}) collective-permute-start(bf16[32,1024]{1,0:T(8,128)(2,1)S(1)} %get-tuple-element.68), channel_id=1, source_target_pairs={{0,2},{1,3},{2,4},{3,5},{4,6},{5,7},{6,0},{7,1},{8,10},{9,11},{10,... | collective-permute-start | bytes 196616 | tf_op jit(solution)/shard_map/ppermute | solution.py:544
  109.2 1.9 %collective-permute-start.20 = (bf16[32,1024]{1,0:T(8,128)(2,1)S(1)}, bf16[32,1024]{1,0:T(8,128)(2,1)S(1)}, u32[]{:S(2)}, u32[]{:S(2)}) collective-permute-start(bf16[32,1024]{1,0:T(8,128)(2,1)S(1)} %get-tuple-element.69), channel_id=1, source_target_pairs={{0,4},{1,5},{2,6},{3,7},{4,0},{5,1},{6,2},{7,3},{8,12},{9,13},{10,... | collective-permute-start | bytes 196616 | tf_op jit(solution)/shard_map/ppermute | solution.py:544
  111.9 3.9 %attention.6 = (f32[64,1024]{1,0:T(8,128)S(1)}, f32[64,1024]{1,0:T(8,128)S(1)}, f32[8,128]{1,0:T(8,128)S(1)}) custom-call(s32[2,32]{1,0:T(2,128)S(1)} %collective-permute-done.refs_3_.refs_0_, f32[1,8]{1,0:T(1,128)S(1)} %copy-done.17, f32[1,8]{1,0:T(1,128)S(1)} %copy-done.18, bf16[128,1024]{1,0:T(8,128)(2,1)S(1)} %get-tuple-element.53.refs_3_, ...), custom_call_target="tpu_custom_call" | custom-call | flops 536870912 | bytes 2097152 | tf_op jit(solution)/shard_map/attention/pallas_call | solution.py:511
  117.0 2.3 %collective-permute-start.24 = (bf16[32,1024]{1,0:T(8,128)(2,1)S(1)}, bf16[32,1024]{1,0:T(8,128)(2,1)S(1)}, u32[]{:S(2)}, u32[]{:S(2)}) collective-permute-start(bf16[32,1024]{1,0:T(8,128)(2,1)S(1)} %chip_sum.1.refs_13_.refs_0_), channel_id=1, source_target_pairs={{0,6},{1,7},{2,0},{3,1},{4,2},{5,3},{6,4},{7,5},{8,14},{9,15},{10,... | collective-permute-start | bytes 196616 | tf_op jit(solution)/shard_map/ppermute | solution.py:544
  121.0 4.7 %attention.7 = (f32[64,1024]{1,0:T(8,128)}, bf16[64,1024]{1,0:T(8,128)(2,1)}, f32[8,128]{1,0:T(8,128)S(1)}) custom-call(s32[2,32]{1,0:T(2,128)S(1)} %collective-permute-done.refs_3_.refs_0_, f32[1,8]{1,0:T(1,128)S(1)} %copy-done.17, f32[1,8]{1,0:T(1,128)S(1)} %copy-done.18, bf16[128,1024]{1,0:T(8,128)(2,1)S(1)} %get-tuple-element.53.refs_3_, ...), custom_call_target="tpu_custom_call" | custom-call | flops 536870912 | bytes 2097152 | tf_op jit(solution)/shard_map/attention/pallas_call | solution.py:511
  127.0 1.5 %collective-permute-done.25.other_ref = bf16[128,1024]{1,0:T(8,128)(2,1)S(1)} collective-permute-done((bf16[128,1024]{1,0:T(8,128)(2,1)S(1)}, bf16[128,1024]{1,0:T(8,128)(2,1)S(1)}, u32[]{:S(2)}, u32[]{:S(2)}) %collective-permute-start.25) | collective-permute-done | bytes 262176 | tf_op jit(solution)/shard_map/ppermute | solution.py:549
  (86 shorter events, 25.0 us)
Async XLA Ops:
  3.3 29.4 %collective-permute-start.4 = (bf16[128,4096]{1,0:T(8,128)(2,1)}, bf16[128,4096]{1,0:T(8,128)(2,1)S(1)}, u32[]{:S(2)}, u32[]{:S(2)}) collective-permute-start(bf16[128,4096]{1,0:T(8,128)(2,1)} %get-tuple-element.45.values_ref.refs_0_), channel_id=1, source_target_pairs={{0,2},{1,3},{2,4},{3,5},{4,6},{5,7},{6,0},{7,1},{8,10},{9,11},{10,... | collective-permute-start | bytes 3145736 | tf_op jit(solution)/shard_map/ppermute | solution.py:544
  16.2 16.5 %collective-permute-start.1 = (bf16[96,1024]{1,0:T(8,128)(2,1)S(1)}, bf16[96,1024]{1,0:T(8,128)(2,1)S(1)}, u32[]{:S(2)}, u32[]{:S(2)}) collective-permute-start(bf16[96,1024]{1,0:T(8,128)(2,1)S(1)} %get-tuple-element.43), channel_id=1, source_target_pairs={{0,1},{1,2},{2,3},{3,4},{4,5},{5,6},{6,7},{8,9},{9,10},{10,11},{11... | collective-permute-start | bytes 589832 | tf_op jit(solution)/shard_map/ppermute | solution.py:538
  17.7 15.0 %collective-permute-start.2 = (bf16[96,1024]{1,0:T(8,128)(2,1)S(1)}, bf16[96,1024]{1,0:T(8,128)(2,1)S(1)}, u32[]{:S(2)}, u32[]{:S(2)}) collective-permute-start(bf16[96,1024]{1,0:T(8,128)(2,1)S(1)} %get-tuple-element.44), channel_id=1, source_target_pairs={{1,0},{2,1},{3,2},{4,3},{5,4},{6,5},{7,6},{9,8},{10,9},{11,10},{12... | collective-permute-start | bytes 589832 | tf_op jit(solution)/shard_map/ppermute | solution.py:538
  19.0 25.4 %collective-permute-start.5 = (bf16[128,1536]{1,0:T(8,128)(2,1)}, bf16[128,1536]{1,0:T(8,128)(2,1)S(1)}, u32[]{:S(2)}, u32[]{:S(2)}) collective-permute-start(bf16[128,1536]{1,0:T(8,128)(2,1)} %get-tuple-element.46), channel_id=1, source_target_pairs={{0,6},{1,7},{2,0},{3,1},{4,2},{5,3},{6,4},{7,5},{8,14},{9,15},{10,... | collective-permute-start | bytes 1179656 | tf_op jit(solution)/shard_map/ppermute | solution.py:544
  24.0 35.2 %collective-permute-start.10 = (bf16[128,2560]{1,0:T(8,128)(2,1)}, bf16[128,2560]{1,0:T(8,128)(2,1)S(1)}, u32[]{:S(2)}, u32[]{:S(2)}) collective-permute-start(bf16[128,2560]{1,0:T(8,128)(2,1)} %get-tuple-element.47), channel_id=1, source_target_pairs={{0,6},{1,7},{2,0},{3,1},{4,2},{5,3},{6,4},{7,5},{8,14},{9,15},{10,... | collective-permute-start | bytes 1966088 | tf_op jit(solution)/shard_map/ppermute | solution.py:544
  32.7 37.7 %collective-permute-start.8 = (bf16[128,2560]{1,0:T(8,128)(2,1)S(1)}, bf16[128,2560]{1,0:T(8,128)(2,1)S(1)}, u32[]{:S(2)}, u32[]{:S(2)}) collective-permute-start(bf16[128,2560]{1,0:T(8,128)(2,1)S(1)} %part_of.7), channel_id=1, source_target_pairs={{0,2},{1,3},{2,4},{3,5},{4,6},{5,7},{6,0},{7,1},{8,10},{9,11},{10,... | collective-permute-start | bytes 1966088 | tf_op jit(solution)/shard_map/ppermute | solution.py:544
  34.0 36.5 %collective-permute-start.3 = (bf16[128,4096]{1,0:T(8,128)(2,1)S(1)}, bf16[128,4096]{1,0:T(8,128)(2,1)S(1)}, u32[]{:S(2)}, u32[]{:S(2)}) collective-permute-start(bf16[128,4096]{1,0:T(8,128)(2,1)S(1)} %part_of.4), channel_id=1, source_target_pairs={{0,1},{1,0},{2,3},{3,2},{4,5},{5,4},{6,7},{7,6},{8,9},{9,8},{10,11... | collective-permute-start | bytes 3145736 | tf_op jit(solution)/shard_map/ppermute | solution.py:549
  44.5 28.7 %collective-permute-start.6 = (bf16[128,4096]{1,0:T(8,128)(2,1)S(1)}, bf16[128,4096]{1,0:T(8,128)(2,1)S(1)}, u32[]{:S(2)}, u32[]{:S(2)}) collective-permute-start(bf16[128,4096]{1,0:T(8,128)(2,1)S(1)} %part_of.5), channel_id=1, source_target_pairs={{0,1},{1,0},{2,3},{3,2},{4,5},{5,4},{6,7},{7,6},{8,9},{9,8},{10,11... | collective-permute-start | bytes 3145736 | tf_op jit(solution)/shard_map/ppermute | solution.py:549
  59.2 12.6 %collective-permute-start.11 = (bf16[128,2560]{1,0:T(8,128)(2,1)S(1)}, bf16[128,2560]{1,0:T(8,128)(2,1)S(1)}, u32[]{:S(2)}, u32[]{:S(2)}) collective-permute-start(bf16[128,2560]{1,0:T(8,128)(2,1)S(1)} %collective-permute-done.10.refs_6_), channel_id=1, source_target_pairs={{0,1},{1,0},{2,3},{3,2},{4,5},{5,4},{6,7},{7,6},{8,9},{9,8},{10,11... | collective-permute-start | bytes 1966088 | tf_op jit(solution)/shard_map/ppermute | solution.py:549
  70.4 3.3 %collective-permute-start.9 = (bf16[128,2560]{1,0:T(8,128)(2,1)S(1)}, bf16[128,2560]{1,0:T(8,128)(2,1)S(1)}, u32[]{:S(2)}, u32[]{:S(2)}) collective-permute-start(bf16[128,2560]{1,0:T(8,128)(2,1)S(1)} %collective-permute-done.8.refs_4_), channel_id=1, source_target_pairs={{0,1},{1,0},{2,3},{3,2},{4,5},{5,4},{6,7},{7,6},{8,9},{9,8},{10,11... | collective-permute-start | bytes 1966088 | tf_op jit(solution)/shard_map/ppermute | solution.py:549
  70.4 13.4 %collective-permute-start.7 = (bf16[128,1536]{1,0:T(8,128)(2,1)S(1)}, bf16[128,1536]{1,0:T(8,128)(2,1)S(1)}, u32[]{:S(2)}, u32[]{:S(2)}) collective-permute-start(bf16[128,1536]{1,0:T(8,128)(2,1)S(1)} %part_of.6), channel_id=1, source_target_pairs={{0,2},{1,3},{2,4},{3,5},{4,6},{5,7},{6,0},{7,1},{8,10},{9,11},{10,... | collective-permute-start | bytes 1179656 | tf_op jit(solution)/shard_map/ppermute | solution.py:544
  70.5 10.7 %collective-permute-start.12 = (bf16[128,1024]{1,0:T(8,128)(2,1)S(1)}, bf16[128,1024]{1,0:T(8,128)(2,1)S(1)}, u32[]{:S(2)}, u32[]{:S(2)}) collective-permute-start(bf16[128,1024]{1,0:T(8,128)(2,1)S(1)} %get-tuple-element.49), channel_id=1, source_target_pairs={{8,0},{16,8},{24,16},{9,1},{17,9},{25,17},{10,2},{18,10},{26,18},{... | collective-permute-start | bytes 786440 | tf_op jit(solution)/shard_map/ppermute | solution.py:538
  71.8 9.4 %collective-permute-start = (s32[2,32]{1,0:T(2,128)S(1)}, s32[2,32]{1,0:T(2,128)S(1)}, u32[]{:S(2)}, u32[]{:S(2)}) collective-permute-start(s32[2,32]{1,0:T(2,128)S(1)} %pad_add_fusion.refs_0_), channel_id=1, source_target_pairs={{8,0},{16,8},{24,16},{9,1},{17,9},{25,17},{10,2},{18,10},{26,18},{... | collective-permute-start | bytes 776 | tf_op jit(solution)/shard_map/ppermute | solution.py:538
  73.2 10.7 %collective-permute-start.14 = (bf16[128,1536]{1,0:T(8,128)(2,1)S(1)}, bf16[128,1536]{1,0:T(8,128)(2,1)S(1)}, u32[]{:S(2)}, u32[]{:S(2)}) collective-permute-start(bf16[128,1536]{1,0:T(8,128)(2,1)S(1)} %collective-permute-done.5.refs_0_.refs_8_.refs_6_), channel_id=1, source_target_pairs={{0,1},{1,0},{2,3},{3,2},{4,5},{5,4},{6,7},{7,6},{8,9},{9,8},{10,11... | collective-permute-start | bytes 1179656 | tf_op jit(solution)/shard_map/ppermute | solution.py:549
  89.9 10.2 %collective-permute-start.15 = (bf16[128,1024]{1,0:T(8,128)(2,1)S(1)}, bf16[128,1024]{1,0:T(8,128)(2,1)S(1)}, u32[]{:S(2)}, u32[]{:S(2)}) collective-permute-start(bf16[128,1024]{1,0:T(8,128)(2,1)S(1)} %attention.5), channel_id=1, source_target_pairs={{8,0},{16,8},{24,16},{9,1},{17,9},{25,17},{10,2},{18,10},{26,18},{... | collective-permute-start | bytes 786440 | tf_op jit(solution)/shard_map/ppermute | solution.py:538
  103.0 3.8 %collective-permute-start.18 = (bf16[128,1024]{1,0:T(8,128)(2,1)S(1)}, bf16[128,1024]{1,0:T(8,128)(2,1)S(1)}, u32[]{:S(2)}, u32[]{:S(2)}) collective-permute-start(bf16[128,1024]{1,0:T(8,128)(2,1)S(1)} %get-tuple-element.63), channel_id=1, source_target_pairs={{0,1},{1,0},{2,3},{3,2},{4,5},{5,4},{6,7},{7,6},{8,9},{9,8},{10,11... | collective-permute-start | bytes 786440 | tf_op jit(solution)/shard_map/ppermute | solution.py:549
  103.1 8.8 %collective-permute-start.16 = (bf16[96,1024]{1,0:T(8,128)(2,1)S(1)}, bf16[96,1024]{1,0:T(8,128)(2,1)S(1)}, u32[]{:S(2)}, u32[]{:S(2)}) collective-permute-start(bf16[96,1024]{1,0:T(8,128)(2,1)S(1)} %get-tuple-element.54), channel_id=1, source_target_pairs={{0,1},{1,2},{2,3},{3,4},{4,5},{5,6},{6,7},{8,9},{9,10},{10,11},{11... | collective-permute-start | bytes 589832 | tf_op jit(solution)/shard_map/ppermute | solution.py:538
  105.5 6.4 %collective-permute-start.17 = (bf16[96,1024]{1,0:T(8,128)(2,1)S(1)}, bf16[96,1024]{1,0:T(8,128)(2,1)S(1)}, u32[]{:S(2)}, u32[]{:S(2)}) collective-permute-start(bf16[96,1024]{1,0:T(8,128)(2,1)S(1)} %get-tuple-element.55), channel_id=1, source_target_pairs={{1,0},{2,1},{3,2},{4,3},{5,4},{6,5},{7,6},{9,8},{10,9},{11,10},{12... | collective-permute-start | bytes 589832 | tf_op jit(solution)/shard_map/ppermute | solution.py:538
  106.9 10.1 %collective-permute-start.19 = (bf16[32,1024]{1,0:T(8,128)(2,1)S(1)}, bf16[32,1024]{1,0:T(8,128)(2,1)S(1)}, u32[]{:S(2)}, u32[]{:S(2)}) collective-permute-start(bf16[32,1024]{1,0:T(8,128)(2,1)S(1)} %get-tuple-element.68), channel_id=1, source_target_pairs={{0,2},{1,3},{2,4},{3,5},{4,6},{5,7},{6,0},{7,1},{8,10},{9,11},{10,... | collective-permute-start | bytes 196616 | tf_op jit(solution)/shard_map/ppermute | solution.py:544
  109.2 7.8 %collective-permute-start.20 = (bf16[32,1024]{1,0:T(8,128)(2,1)S(1)}, bf16[32,1024]{1,0:T(8,128)(2,1)S(1)}, u32[]{:S(2)}, u32[]{:S(2)}) collective-permute-start(bf16[32,1024]{1,0:T(8,128)(2,1)S(1)} %get-tuple-element.69), channel_id=1, source_target_pairs={{0,4},{1,5},{2,6},{3,7},{4,0},{5,1},{6,2},{7,3},{8,12},{9,13},{10,... | collective-permute-start | bytes 196616 | tf_op jit(solution)/shard_map/ppermute | solution.py:544
  111.1 5.8 %collective-permute-start.21 = (bf16[32,1024]{1,0:T(8,128)(2,1)S(1)}, bf16[32,1024]{1,0:T(8,128)(2,1)S(1)}, u32[]{:S(2)}, u32[]{:S(2)}) collective-permute-start(bf16[32,1024]{1,0:T(8,128)(2,1)S(1)} %get-tuple-element.70), channel_id=1, source_target_pairs={{0,6},{1,7},{2,0},{3,1},{4,2},{5,3},{6,4},{7,5},{8,14},{9,15},{10,... | collective-permute-start | bytes 196616 | tf_op jit(solution)/shard_map/ppermute | solution.py:544
  117.0 8.7 %collective-permute-start.24 = (bf16[32,1024]{1,0:T(8,128)(2,1)S(1)}, bf16[32,1024]{1,0:T(8,128)(2,1)S(1)}, u32[]{:S(2)}, u32[]{:S(2)}) collective-permute-start(bf16[32,1024]{1,0:T(8,128)(2,1)S(1)} %chip_sum.1.refs_13_.refs_0_), channel_id=1, source_target_pairs={{0,6},{1,7},{2,0},{3,1},{4,2},{5,3},{6,4},{7,5},{8,14},{9,15},{10,... | collective-permute-start | bytes 196616 | tf_op jit(solution)/shard_map/ppermute | solution.py:544
  119.3 7.6 %collective-permute-start.23 = (bf16[32,1024]{1,0:T(8,128)(2,1)S(1)}, bf16[32,1024]{1,0:T(8,128)(2,1)S(1)}, u32[]{:S(2)}, u32[]{:S(2)}) collective-permute-start(bf16[32,1024]{1,0:T(8,128)(2,1)S(1)} %chip_sum.1.refs_13_.refs_0_), channel_id=1, source_target_pairs={{0,4},{1,5},{2,6},{3,7},{4,0},{5,1},{6,2},{7,3},{8,12},{9,13},{10,... | collective-permute-start | bytes 196616 | tf_op jit(solution)/shard_map/ppermute | solution.py:544
  120.2 6.7 %collective-permute-start.22 = (bf16[32,1024]{1,0:T(8,128)(2,1)S(1)}, bf16[32,1024]{1,0:T(8,128)(2,1)S(1)}, u32[]{:S(2)}, u32[]{:S(2)}) collective-permute-start(bf16[32,1024]{1,0:T(8,128)(2,1)S(1)} %chip_sum.1.refs_13_.refs_0_), channel_id=1, source_target_pairs={{0,2},{1,3},{2,4},{3,5},{4,6},{5,7},{6,0},{7,1},{8,10},{9,11},{10,... | collective-permute-start | bytes 196616 | tf_op jit(solution)/shard_map/ppermute | solution.py:544
  (21 other events, 164.4 us)
where the time goes:
time: 130 us; the launch traced here: 129 us
  waiting for transfers between devices  60.1 us (46%)
  starting transfers between devices  33.3 us (26%)
  Pallas kernels  26.2 us (20%)
  local copies, waits for them, and re-layouts  8.25 us (6%)
    ppermute x11, waiting for transfers between devices, rotated(): return lax.ppermute(values, 'tok', pairs)  44.7 us
    ppermute x11, starting transfers between devices, rotated(): return lax.ppermute(values, 'tok', pairs)  19 us
    pallas_call x4, Pallas kernels, attention(): pl.pallas_call(functools.partial(attention_kernel, pairs, first_pair, par...  16.6 us
    ppermute x7, waiting for transfers between devices, shifted(): return lax.ppermute(values, axis, pairs)  12.1 us
    ppermute x7, starting transfers between devices, shifted(): return lax.ppermute(values, axis, pairs)  10.3 us
    unnamed x38, local copies, waits for them, and re-layouts  8.25 us
    pallas_call x2, Pallas kernels, adapter(): pl.pallas_call(functools.partial(adapter_kernel, packed), out_shape=outs,...  4.55 us
    ppermute x8, starting transfers between devices, swapped(): return lax.ppermute(values, 'tok', [(i, i ^ 1) for i in range(devices)])  3.9 us
  transfers between devices with their start and end apart: 26, of which 11 were waited for; matrix products, arithmetic and copies ran while one was open for 1% of the time, Pallas kernels for 12%

commit v1 on v0

--- a/solution.py
+++ b/solution.py
@@ -454,7 +454,7 @@
             qb, kb = qn.astype(jnp.bfloat16), kn.astype(jnp.bfloat16)
             score = contract_last(qb, kb) * factor - slope_ref[0, head] * logs_now
             weights = jnp.where(logs_now >= 0.0, jnp.exp(score), 0.0)
-            prob = weights / jnp.sum(weights, axis=-1, keepdims=True)
+            prob = weights * (1.0 / jnp.sum(weights, axis=-1, keepdims=True))
             prob_bf = prob.astype(jnp.bfloat16)
             mixed.append(dot(prob_bf[:rows], vb).astype(jnp.bfloat16))
             dprob = contract_last(dob, vb)
@@ -470,7 +470,7 @@
             dk_all.append(dk.astype(jnp.bfloat16))
             dv_all.append(dv.astype(jnp.bfloat16))
         top_acc[...] += dot(jnp.concatenate(mixed, axis=1), wo_now[...])
-        nf_acc[...] += contract_last(jnp.concatenate(dq_all + dk_all + dv_all, axis=1), w_now[...])
+        nf_acc[...] += contract_last(w_now[...], jnp.concatenate(dq_all + dk_all + dv_all, axis=1))
 
     if ends != "one":
         done_ref[...] = jnp.zeros_like(done_ref)
@@ -484,7 +484,7 @@
         top, bottom_cot = late_ref[:rows], late_ref[rows:]
     top = top.astype(jnp.float32) - top_acc[...]
     scaled, inverse = normalised(bottom_ref[...])
-    back = norm_back(nf_acc[...], gain_ref[...], scaled, inverse)
+    back = norm_back(nf_acc[...].T, gain_ref[...], scaled, inverse)
     cot = (bottom_cot.astype(jnp.float32) + back).astype(jnp.bfloat16)
     if ends == "one":
         send_ref[:rows] = top.astype(jnp.bfloat16)
@@ -505,7 +505,7 @@
     elif ends == "two":
         outs = (own_rows, jax.ShapeDtypeStruct((rows, width), bf))
     else:
-        outs = (own_rows, own_rows)
+        outs = (own_rows, jax.ShapeDtypeStruct((width, rows), jnp.float32))
     if ends != "one":
         outs += (jax.ShapeDtypeStruct((8, 128), jnp.float32),)
     return pl.pallas_call(
@@ -520,7 +520,7 @@
             pltpu.VMEM((rows + 2 * WIN, width), bf),
             pltpu.VMEM((rows + 2 * WIN, 3 * rows), jnp.float32),
             pltpu.VMEM((rows, width), jnp.float32),
-            pltpu.VMEM((rows, width), jnp.float32),
+            pltpu.VMEM((width, rows), jnp.float32),
         ],
         compiler_params=pltpu.CompilerParams(vmem_limit_bytes=LARGE),
         cost_estimate=pl.CostEstimate(

time: 130 us -> 130 us (level)
  no operation moved by 1% of the time
where the time goes in v1:
time: 130 us
  waiting for transfers between devices  59.8 us (46%)
  starting transfers between devices  33.3 us (26%)
  Pallas kernels  26.7 us (21%)
  local copies, waits for them, and re-layouts  8.25 us (6%)
    ppermute x11, waiting for transfers between devices, rotated(): return lax.ppermute(values, 'tok', pairs)  44.6 us
    ppermute x11, starting transfers between devices, rotated(): return lax.ppermute(values, 'tok', pairs)  19 us
    pallas_call x4, Pallas kernels, attention(): pl.pallas_call(functools.partial(attention_kernel, pairs, first_pair, par...  17.1 us
    ppermute x7, waiting for transfers between devices, shifted(): return lax.ppermute(values, axis, pairs)  12 us
    ppermute x7, starting transfers between devices, shifted(): return lax.ppermute(values, axis, pairs)  10.3 us
    unnamed x38, local copies, waits for them, and re-layouts  8.25 us
    pallas_call x2, Pallas kernels, adapter(): pl.pallas_call(functools.partial(adapter_kernel, packed), out_shape=outs,...  4.55 us
    ppermute x8, starting transfers between devices, swapped(): return lax.ppermute(values, 'tok', [(i, i ^ 1) for i in range(devices)])  3.9 us
  transfers between devices with their start and end apart: 26, of which 11 were waited for; matrix products, arithmetic and copies ran while one was open for 1% of the time, Pallas kernels for 12%

profile of v1, /device:TPU:0, one launch (start us, length us, event | category | flops | bytes accessed | tf_op | source)
XLA Modules:
  0.0 129.7 jit_solution(14640402366782143620)
XLA Ops:
  0.6 2.6 %arrange.1 = (bf16[128,4096]{1,0:T(8,128)(2,1)}, bf16[128,2560]{1,0:T(8,128)(2,1)}, bf16[128,1536]{1,0:T(8,128)(2,1)}) custom-call(bf16[128,3072]{1,0:T(8,128)(2,1)} %bitcast.26, bf16[128,1024]{1,0:T(8,128)(2,1)} %bitcast.27), custom_call_target="tpu_custom_call" | custom-call | tf_op jit(solution)/shard_map/arrange/pallas_call | solution.py:296
  3.3 3.1 %collective-permute-start.4 = (bf16[128,4096]{1,0:T(8,128)(2,1)}, bf16[128,4096]{1,0:T(8,128)(2,1)S(1)}, u32[]{:S(2)}, u32[]{:S(2)}) collective-permute-start(bf16[128,4096]{1,0:T(8,128)(2,1)} %get-tuple-element.45.values_ref.refs_0_), channel_id=1, source_target_pairs={{0,2},{1,3},{2,4},{3,5},{4,6},{5,7},{6,0},{7,1},{8,10},{9,11},{10,... | collective-permute-start | bytes 3145736 | tf_op jit(solution)/shard_map/ppermute | solution.py:544
  14.0 2.2 %adapter.2 = (f32[64,1024]{1,0:T(8,128)S(1)}, bf16[64,1024]{1,0:T(8,128)(2,1)}, bf16[96,1024]{1,0:T(8,128)(2,1)S(1)}, bf16[96,1024]{1,0:T(8,128)(2,1)S(1)}, bf16...) custom-call(s32[2,32]{1,0:T(2,128)S(1)} %pad_add_fusion.refs_0_, ...), custom_call_target="tpu_custom_call" | custom-call | flops 67108864 | bytes 1310720 | tf_op jit(solution)/shard_map/adapter/pallas_call | solution.py:128
  19.0 5.0 %collective-permute-start.5 = (bf16[128,1536]{1,0:T(8,128)(2,1)}, bf16[128,1536]{1,0:T(8,128)(2,1)S(1)}, u32[]{:S(2)}, u32[]{:S(2)}) collective-permute-start(bf16[128,1536]{1,0:T(8,128)(2,1)} %get-tuple-element.46), channel_id=1, source_target_pairs={{0,6},{1,7},{2,0},{3,1},{4,2},{5,3},{6,4},{7,5},{8,14},{9,15},{10,... | collective-permute-start | bytes 1179656 | tf_op jit(solution)/shard_map/ppermute | solution.py:544
  24.0 1.9 %collective-permute-start.10 = (bf16[128,2560]{1,0:T(8,128)(2,1)}, bf16[128,2560]{1,0:T(8,128)(2,1)S(1)}, u32[]{:S(2)}, u32[]{:S(2)}) collective-permute-start(bf16[128,2560]{1,0:T(8,128)(2,1)} %get-tuple-element.47), channel_id=1, source_target_pairs={{0,6},{1,7},{2,0},{3,1},{4,2},{5,3},{6,4},{7,5},{8,14},{9,15},{10,... | collective-permute-start | bytes 1966088 | tf_op jit(solution)/shard_map/ppermute | solution.py:544
  25.9 6.7 %collective-permute-done.4.values_ref.refs_2_ = bf16[128,4096]{1,0:T(8,128)(2,1)S(1)} collective-permute-done((bf16[128,4096]{1,0:T(8,128)(2,1)}, bf16[128,4096]{1,0:T(8,128)(2,1)S(1)}, u32[]{:S(2)}, u32[]{:S(2)}) %collective-permute-start.4) | collective-permute-done | bytes 1048608 | tf_op jit(solution)/shard_map/ppermute | solution.py:544
  34.0 3.1 %collective-permute-start.3 = (bf16[128,4096]{1,0:T(8,128)(2,1)S(1)}, bf16[128,4096]{1,0:T(8,128)(2,1)S(1)}, u32[]{:S(2)}, u32[]{:S(2)}) collective-permute-start(bf16[128,4096]{1,0:T(8,128)(2,1)S(1)} %part_of.4), channel_id=1, source_target_pairs={{0,1},{1,0},{2,3},{3,2},{4,5},{5,4},{6,7},{7,6},{8,9},{9,8},{10,11... | collective-permute-start | bytes 3145736 | tf_op jit(solution)/shard_map/ppermute | solution.py:549
  37.1 7.2 %collective-permute-done.5.refs_0_.refs_8_.refs_6_ = bf16[128,1536]{1,0:T(8,128)(2,1)S(1)} collective-permute-done((bf16[128,1536]{1,0:T(8,128)(2,1)}, bf16[128,1536]{1,0:T(8,128)(2,1)S(1)}, u32[]{:S(2)}, u32[]{:S(2)}) %collective-permute-start.5) | collective-permute-done | bytes 393248 | tf_op jit(solution)/shard_map/ppermute | solution.py:544
  44.5 14.7 %collective-permute-done.10.refs_6_ = bf16[128,2560]{1,0:T(8,128)(2,1)S(1)} collective-permute-done((bf16[128,2560]{1,0:T(8,128)(2,1)}, bf16[128,2560]{1,0:T(8,128)(2,1)S(1)}, u32[]{:S(2)}, u32[]{:S(2)}) %collective-permute-start.10) | collective-permute-done | bytes 655392 | tf_op jit(solution)/shard_map/ppermute | solution.py:544
  59.2 11.2 %collective-permute-done.8.refs_4_ = bf16[128,2560]{1,0:T(8,128)(2,1)S(1)} collective-permute-done((bf16[128,2560]{1,0:T(8,128)(2,1)S(1)}, bf16[128,2560]{1,0:T(8,128)(2,1)S(1)}, u32[]{:S(2)}, u32[]{:S(2)}) %collective-permute-start.8) | collective-permute-done | bytes 655392 | tf_op jit(solution)/shard_map/ppermute | solution.py:544
  74.1 4.0 %attention.4 = (f32[64,1024]{1,0:T(8,128)S(1)}, f32[1024,64]{1,0:T(8,128)S(1)}, f32[8,128]{1,0:T(8,128)S(1)}) custom-call(s32[2,32]{1,0:T(2,128)S(1)} %pad_add_fusion.refs_0_, f32[1,8]{1,0:T(1,128)S(1)} %copy-done.17, f32[1,8]{1,0:T(1,128)S(1)} %copy-done.18, bf16[128,1024]{1,0:T(8,128)(2,1)S(1)} %get-tuple-element.42.refs_0_.refs_1_.refs_3_, ...), custom_call_target="tpu_custom_call" | custom-call | flops 536870912 | bytes 2097152 | tf_op jit(solution)/shard_map/attention/pallas_call | solution.py:511
  78.2 3.0 %collective-permute-done.refs_3_.refs_0_ = s32[2,32]{1,0:T(2,128)S(1)} collective-permute-done((s32[2,32]{1,0:T(2,128)S(1)}, s32[2,32]{1,0:T(2,128)S(1)}, u32[]{:S(2)}, u32[]{:S(2)}) %collective-permute-start) | collective-permute-done | bytes 288 | tf_op jit(solution)/shard_map/ppermute | solution.py:538
  81.2 2.6 %collective-permute-done.7.refs_0_ = bf16[128,1536]{1,0:T(8,128)(2,1)S(1)} collective-permute-done((bf16[128,1536]{1,0:T(8,128)(2,1)S(1)}, bf16[128,1536]{1,0:T(8,128)(2,1)S(1)}, u32[]{:S(2)}, u32[]{:S(2)}) %collective-permute-start.7) | collective-permute-done | bytes 393248 | tf_op jit(solution)/shard_map/ppermute | solution.py:544
  83.8 1.7 %collective-permute-done.13.refs_5_ = bf16[128,1536]{1,0:T(8,128)(2,1)S(1)} collective-permute-done((bf16[128,1536]{1,0:T(8,128)(2,1)S(1)}, bf16[128,1536]{1,0:T(8,128)(2,1)S(1)}, u32[]{:S(2)}, u32[]{:S(2)}) %collective-permute-start.13) | collective-permute-done | bytes 393248 | tf_op jit(solution)/shard_map/ppermute | solution.py:549
  85.8 4.2 %attention.5 = bf16[128,1024]{1,0:T(8,128)(2,1)S(1)} custom-call(s32[2,32]{1,0:T(2,128)S(1)} %pad_add_fusion.refs_0_, f32[1,8]{1,0:T(1,128)S(1)} %copy-done.17, f32[1,8]{1,0:T(1,128)S(1)} %copy-done.18, bf16[128,1024]{1,0:T(8,128)(2,1)S(1)} %get-tuple-element.42.refs_0_.refs_1_.refs_3_, bf16[96,1024]{1,0:T(8,128)(2,1)S(1)} %collective-permute-done.1.refs_0_.refs_4_, ...), custom_call_target="tpu_custom_call" | custom-call | flops 536870912 | bytes 2097152 | tf_op jit(solution)/shard_map/attention/pallas_call | solution.py:511
  91.3 8.9 %collective-permute-done.15.refs_1_.late_ref.refs_10_ = bf16[128,1024]{1,0:T(8,128)(2,1)S(1)} collective-permute-done((bf16[128,1024]{1,0:T(8,128)(2,1)S(1)}, bf16[128,1024]{1,0:T(8,128)(2,1)S(1)}, u32[]{:S(2)}, u32[]{:S(2)}) %collective-permute-start.15) | collective-permute-done | bytes 262176 | tf_op jit(solution)/shard_map/ppermute | solution.py:538
  100.3 2.3 %adapter.3 = (f32[64,1024]{1,0:T(8,128)}, bf16[64,1024]{1,0:T(8,128)(2,1)}, bf16[96,1024]{1,0:T(8,128)(2,1)S(1)}, bf16[96,1024]{1,0:T(8,128)(2,1)S(1)}, bf16[128...) custom-call(s32[2,32]{1,0:T(2,128)S(1)} %collective-permute-done.ref, ...), custom_call_target="tpu_custom_call" | custom-call | flops 67108864 | bytes 1310720 | tf_op jit(solution)/shard_map/adapter/pallas_call | solution.py:128
  103.2 2.4 %collective-permute-start.16 = (bf16[96,1024]{1,0:T(8,128)(2,1)S(1)}, bf16[96,1024]{1,0:T(8,128)(2,1)S(1)}, u32[]{:S(2)}, u32[]{:S(2)}) collective-permute-start(bf16[96,1024]{1,0:T(8,128)(2,1)S(1)} %get-tuple-element.54), channel_id=1, source_target_pairs={{0,1},{1,2},{2,3},{3,4},{4,5},{5,6},{6,7},{8,9},{9,10},{10,11},{11... | collective-permute-start | bytes 589832 | tf_op jit(solution)/shard_map/ppermute | solution.py:538
  107.0 2.3 %collective-permute-start.19 = (bf16[32,1024]{1,0:T(8,128)(2,1)S(1)}, bf16[32,1024]{1,0:T(8,128)(2,1)S(1)}, u32[]{:S(2)}, u32[]{:S(2)}) collective-permute-start(bf16[32,1024]{1,0:T(8,128)(2,1)S(1)} %get-tuple-element.68), channel_id=1, source_target_pairs={{0,2},{1,3},{2,4},{3,5},{4,6},{5,7},{6,0},{7,1},{8,10},{9,11},{10,... | collective-permute-start | bytes 196616 | tf_op jit(solution)/shard_map/ppermute | solution.py:544
  109.3 1.9 %collective-permute-start.20 = (bf16[32,1024]{1,0:T(8,128)(2,1)S(1)}, bf16[32,1024]{1,0:T(8,128)(2,1)S(1)}, u32[]{:S(2)}, u32[]{:S(2)}) collective-permute-start(bf16[32,1024]{1,0:T(8,128)(2,1)S(1)} %get-tuple-element.69), channel_id=1, source_target_pairs={{0,4},{1,5},{2,6},{3,7},{4,0},{5,1},{6,2},{7,3},{8,12},{9,13},{10,... | collective-permute-start | bytes 196616 | tf_op jit(solution)/shard_map/ppermute | solution.py:544
  112.1 4.0 %attention.6 = (f32[64,1024]{1,0:T(8,128)S(1)}, f32[1024,64]{1,0:T(8,128)S(1)}, f32[8,128]{1,0:T(8,128)S(1)}) custom-call(s32[2,32]{1,0:T(2,128)S(1)} %collective-permute-done.refs_3_.refs_0_, f32[1,8]{1,0:T(1,128)S(1)} %copy-done.17, f32[1,8]{1,0:T(1,128)S(1)} %copy-done.18, bf16[128,1024]{1,0:T(8,128)(2,1)S(1)} %get-tuple-element.53.refs_3_, ...), custom_call_target="tpu_custom_call" | custom-call | flops 536870912 | bytes 2097152 | tf_op jit(solution)/shard_map/attention/pallas_call | solution.py:511
  117.1 2.4 %collective-permute-start.24 = (bf16[32,1024]{1,0:T(8,128)(2,1)S(1)}, bf16[32,1024]{1,0:T(8,128)(2,1)S(1)}, u32[]{:S(2)}, u32[]{:S(2)}) collective-permute-start(bf16[32,1024]{1,0:T(8,128)(2,1)S(1)} %chip_sum.1.refs_13_.refs_0_), channel_id=1, source_target_pairs={{0,6},{1,7},{2,0},{3,1},{4,2},{5,3},{6,4},{7,5},{8,14},{9,15},{10,... | collective-permute-start | bytes 196616 | tf_op jit(solution)/shard_map/ppermute | solution.py:544
  121.1 4.8 %attention.7 = (f32[64,1024]{1,0:T(8,128)}, bf16[64,1024]{1,0:T(8,128)(2,1)}, f32[8,128]{1,0:T(8,128)S(1)}) custom-call(s32[2,32]{1,0:T(2,128)S(1)} %collective-permute-done.refs_3_.refs_0_, f32[1,8]{1,0:T(1,128)S(1)} %copy-done.17, f32[1,8]{1,0:T(1,128)S(1)} %copy-done.18, bf16[128,1024]{1,0:T(8,128)(2,1)S(1)} %get-tuple-element.53.refs_3_, ...), custom_call_target="tpu_custom_call" | custom-call | flops 536870912 | bytes 2097152 | tf_op jit(solution)/shard_map/attention/pallas_call | solution.py:511
  127.3 1.5 %collective-permute-done.25.other_ref = bf16[128,1024]{1,0:T(8,128)(2,1)S(1)} collective-permute-done((bf16[128,1024]{1,0:T(8,128)(2,1)S(1)}, bf16[128,1024]{1,0:T(8,128)(2,1)S(1)}, u32[]{:S(2)}, u32[]{:S(2)}) %collective-permute-start.25) | collective-permute-done | bytes 262176 | tf_op jit(solution)/shard_map/ppermute | solution.py:549
  (86 shorter events, 24.8 us)
Async XLA Ops:
  3.3 29.4 %collective-permute-start.4 = (bf16[128,4096]{1,0:T(8,128)(2,1)}, bf16[128,4096]{1,0:T(8,128)(2,1)S(1)}, u32[]{:S(2)}, u32[]{:S(2)}) collective-permute-start(bf16[128,4096]{1,0:T(8,128)(2,1)} %get-tuple-element.45.values_ref.refs_0_), channel_id=1, source_target_pairs={{0,2},{1,3},{2,4},{3,5},{4,6},{5,7},{6,0},{7,1},{8,10},{9,11},{10,... | collective-permute-start | bytes 3145736 | tf_op jit(solution)/shard_map/ppermute | solution.py:544
  16.2 16.5 %collective-permute-start.1 = (bf16[96,1024]{1,0:T(8,128)(2,1)S(1)}, bf16[96,1024]{1,0:T(8,128)(2,1)S(1)}, u32[]{:S(2)}, u32[]{:S(2)}) collective-permute-start(bf16[96,1024]{1,0:T(8,128)(2,1)S(1)} %get-tuple-element.43), channel_id=1, source_target_pairs={{0,1},{1,2},{2,3},{3,4},{4,5},{5,6},{6,7},{8,9},{9,10},{10,11},{11... | collective-permute-start | bytes 589832 | tf_op jit(solution)/shard_map/ppermute | solution.py:538
  17.7 15.0 %collective-permute-start.2 = (bf16[96,1024]{1,0:T(8,128)(2,1)S(1)}, bf16[96,1024]{1,0:T(8,128)(2,1)S(1)}, u32[]{:S(2)}, u32[]{:S(2)}) collective-permute-start(bf16[96,1024]{1,0:T(8,128)(2,1)S(1)} %get-tuple-element.44), channel_id=1, source_target_pairs={{1,0},{2,1},{3,2},{4,3},{5,4},{6,5},{7,6},{9,8},{10,9},{11,10},{12... | collective-permute-start | bytes 589832 | tf_op jit(solution)/shard_map/ppermute | solution.py:538
  19.0 25.4 %collective-permute-start.5 = (bf16[128,1536]{1,0:T(8,128)(2,1)}, bf16[128,1536]{1,0:T(8,128)(2,1)S(1)}, u32[]{:S(2)}, u32[]{:S(2)}) collective-permute-start(bf16[128,1536]{1,0:T(8,128)(2,1)} %get-tuple-element.46), channel_id=1, source_target_pairs={{0,6},{1,7},{2,0},{3,1},{4,2},{5,3},{6,4},{7,5},{8,14},{9,15},{10,... | collective-permute-start | bytes 1179656 | tf_op jit(solution)/shard_map/ppermute | solution.py:544
  24.0 35.2 %collective-permute-start.10 = (bf16[128,2560]{1,0:T(8,128)(2,1)}, bf16[128,2560]{1,0:T(8,128)(2,1)S(1)}, u32[]{:S(2)}, u32[]{:S(2)}) collective-permute-start(bf16[128,2560]{1,0:T(8,128)(2,1)} %get-tuple-element.47), channel_id=1, source_target_pairs={{0,6},{1,7},{2,0},{3,1},{4,2},{5,3},{6,4},{7,5},{8,14},{9,15},{10,... | collective-permute-start | bytes 1966088 | tf_op jit(solution)/shard_map/ppermute | solution.py:544
  32.7 37.7 %collective-permute-start.8 = (bf16[128,2560]{1,0:T(8,128)(2,1)S(1)}, bf16[128,2560]{1,0:T(8,128)(2,1)S(1)}, u32[]{:S(2)}, u32[]{:S(2)}) collective-permute-start(bf16[128,2560]{1,0:T(8,128)(2,1)S(1)} %part_of.7), channel_id=1, source_target_pairs={{0,2},{1,3},{2,4},{3,5},{4,6},{5,7},{6,0},{7,1},{8,10},{9,11},{10,... | collective-permute-start | bytes 1966088 | tf_op jit(solution)/shard_map/ppermute | solution.py:544
  34.0 36.5 %collective-permute-start.3 = (bf16[128,4096]{1,0:T(8,128)(2,1)S(1)}, bf16[128,4096]{1,0:T(8,128)(2,1)S(1)}, u32[]{:S(2)}, u32[]{:S(2)}) collective-permute-start(bf16[128,4096]{1,0:T(8,128)(2,1)S(1)} %part_of.4), channel_id=1, source_target_pairs={{0,1},{1,0},{2,3},{3,2},{4,5},{5,4},{6,7},{7,6},{8,9},{9,8},{10,11... | collective-permute-start | bytes 3145736 | tf_op jit(solution)/shard_map/ppermute | solution.py:549
  44.5 28.7 %collective-permute-start.6 = (bf16[128,4096]{1,0:T(8,128)(2,1)S(1)}, bf16[128,4096]{1,0:T(8,128)(2,1)S(1)}, u32[]{:S(2)}, u32[]{:S(2)}) collective-permute-start(bf16[128,4096]{1,0:T(8,128)(2,1)S(1)} %part_of.5), channel_id=1, source_target_pairs={{0,1},{1,0},{2,3},{3,2},{4,5},{5,4},{6,7},{7,6},{8,9},{9,8},{10,11... | collective-permute-start | bytes 3145736 | tf_op jit(solution)/shard_map/ppermute | solution.py:549
  59.2 12.6 %collective-permute-start.11 = (bf16[128,2560]{1,0:T(8,128)(2,1)S(1)}, bf16[128,2560]{1,0:T(8,128)(2,1)S(1)}, u32[]{:S(2)}, u32[]{:S(2)}) collective-permute-start(bf16[128,2560]{1,0:T(8,128)(2,1)S(1)} %collective-permute-done.10.refs_6_), channel_id=1, source_target_pairs={{0,1},{1,0},{2,3},{3,2},{4,5},{5,4},{6,7},{7,6},{8,9},{9,8},{10,11... | collective-permute-start | bytes 1966088 | tf_op jit(solution)/shard_map/ppermute | solution.py:549
  70.4 3.3 %collective-permute-start.9 = (bf16[128,2560]{1,0:T(8,128)(2,1)S(1)}, bf16[128,2560]{1,0:T(8,128)(2,1)S(1)}, u32[]{:S(2)}, u32[]{:S(2)}) collective-permute-start(bf16[128,2560]{1,0:T(8,128)(2,1)S(1)} %collective-permute-done.8.refs_4_), channel_id=1, source_target_pairs={{0,1},{1,0},{2,3},{3,2},{4,5},{5,4},{6,7},{7,6},{8,9},{9,8},{10,11... | collective-permute-start | bytes 1966088 | tf_op jit(solution)/shard_map/ppermute | solution.py:549
  70.4 13.4 %collective-permute-start.7 = (bf16[128,1536]{1,0:T(8,128)(2,1)S(1)}, bf16[128,1536]{1,0:T(8,128)(2,1)S(1)}, u32[]{:S(2)}, u32[]{:S(2)}) collective-permute-start(bf16[128,1536]{1,0:T(8,128)(2,1)S(1)} %part_of.6), channel_id=1, source_target_pairs={{0,2},{1,3},{2,4},{3,5},{4,6},{5,7},{6,0},{7,1},{8,10},{9,11},{10,... | collective-permute-start | bytes 1179656 | tf_op jit(solution)/shard_map/ppermute | solution.py:544
  70.5 10.7 %collective-permute-start.12 = (bf16[128,1024]{1,0:T(8,128)(2,1)S(1)}, bf16[128,1024]{1,0:T(8,128)(2,1)S(1)}, u32[]{:S(2)}, u32[]{:S(2)}) collective-permute-start(bf16[128,1024]{1,0:T(8,128)(2,1)S(1)} %get-tuple-element.49), channel_id=1, source_target_pairs={{8,0},{16,8},{24,16},{9,1},{17,9},{25,17},{10,2},{18,10},{26,18},{... | collective-permute-start | bytes 786440 | tf_op jit(solution)/shard_map/ppermute | solution.py:538
  71.8 9.4 %collective-permute-start = (s32[2,32]{1,0:T(2,128)S(1)}, s32[2,32]{1,0:T(2,128)S(1)}, u32[]{:S(2)}, u32[]{:S(2)}) collective-permute-start(s32[2,32]{1,0:T(2,128)S(1)} %pad_add_fusion.refs_0_), channel_id=1, source_target_pairs={{8,0},{16,8},{24,16},{9,1},{17,9},{25,17},{10,2},{18,10},{26,18},{... | collective-permute-start | bytes 776 | tf_op jit(solution)/shard_map/ppermute | solution.py:538
  73.2 10.7 %collective-permute-start.14 = (bf16[128,1536]{1,0:T(8,128)(2,1)S(1)}, bf16[128,1536]{1,0:T(8,128)(2,1)S(1)}, u32[]{:S(2)}, u32[]{:S(2)}) collective-permute-start(bf16[128,1536]{1,0:T(8,128)(2,1)S(1)} %collective-permute-done.5.refs_0_.refs_8_.refs_6_), channel_id=1, source_target_pairs={{0,1},{1,0},{2,3},{3,2},{4,5},{5,4},{6,7},{7,6},{8,9},{9,8},{10,11... | collective-permute-start | bytes 1179656 | tf_op jit(solution)/shard_map/ppermute | solution.py:549
  90.0 10.2 %collective-permute-start.15 = (bf16[128,1024]{1,0:T(8,128)(2,1)S(1)}, bf16[128,1024]{1,0:T(8,128)(2,1)S(1)}, u32[]{:S(2)}, u32[]{:S(2)}) collective-permute-start(bf16[128,1024]{1,0:T(8,128)(2,1)S(1)} %attention.5), channel_id=1, source_target_pairs={{8,0},{16,8},{24,16},{9,1},{17,9},{25,17},{10,2},{18,10},{26,18},{... | collective-permute-start | bytes 786440 | tf_op jit(solution)/shard_map/ppermute | solution.py:538
  103.2 3.8 %collective-permute-start.18 = (bf16[128,1024]{1,0:T(8,128)(2,1)S(1)}, bf16[128,1024]{1,0:T(8,128)(2,1)S(1)}, u32[]{:S(2)}, u32[]{:S(2)}) collective-permute-start(bf16[128,1024]{1,0:T(8,128)(2,1)S(1)} %get-tuple-element.63), channel_id=1, source_target_pairs={{0,1},{1,0},{2,3},{3,2},{4,5},{5,4},{6,7},{7,6},{8,9},{9,8},{10,11... | collective-permute-start | bytes 786440 | tf_op jit(solution)/shard_map/ppermute | solution.py:549
  103.2 8.8 %collective-permute-start.16 = (bf16[96,1024]{1,0:T(8,128)(2,1)S(1)}, bf16[96,1024]{1,0:T(8,128)(2,1)S(1)}, u32[]{:S(2)}, u32[]{:S(2)}) collective-permute-start(bf16[96,1024]{1,0:T(8,128)(2,1)S(1)} %get-tuple-element.54), channel_id=1, source_target_pairs={{0,1},{1,2},{2,3},{3,4},{4,5},{5,6},{6,7},{8,9},{9,10},{10,11},{11... | collective-permute-start | bytes 589832 | tf_op jit(solution)/shard_map/ppermute | solution.py:538
  105.6 6.4 %collective-permute-start.17 = (bf16[96,1024]{1,0:T(8,128)(2,1)S(1)}, bf16[96,1024]{1,0:T(8,128)(2,1)S(1)}, u32[]{:S(2)}, u32[]{:S(2)}) collective-permute-start(bf16[96,1024]{1,0:T(8,128)(2,1)S(1)} %get-tuple-element.55), channel_id=1, source_target_pairs={{1,0},{2,1},{3,2},{4,3},{5,4},{6,5},{7,6},{9,8},{10,9},{11,10},{12... | collective-permute-start | bytes 589832 | tf_op jit(solution)/shard_map/ppermute | solution.py:538
  107.0 10.1 %collective-permute-start.19 = (bf16[32,1024]{1,0:T(8,128)(2,1)S(1)}, bf16[32,1024]{1,0:T(8,128)(2,1)S(1)}, u32[]{:S(2)}, u32[]{:S(2)}) collective-permute-start(bf16[32,1024]{1,0:T(8,128)(2,1)S(1)} %get-tuple-element.68), channel_id=1, source_target_pairs={{0,2},{1,3},{2,4},{3,5},{4,6},{5,7},{6,0},{7,1},{8,10},{9,11},{10,... | collective-permute-start | bytes 196616 | tf_op jit(solution)/shard_map/ppermute | solution.py:544
  109.3 7.8 %collective-permute-start.20 = (bf16[32,1024]{1,0:T(8,128)(2,1)S(1)}, bf16[32,1024]{1,0:T(8,128)(2,1)S(1)}, u32[]{:S(2)}, u32[]{:S(2)}) collective-permute-start(bf16[32,1024]{1,0:T(8,128)(2,1)S(1)} %get-tuple-element.69), channel_id=1, source_target_pairs={{0,4},{1,5},{2,6},{3,7},{4,0},{5,1},{6,2},{7,3},{8,12},{9,13},{10,... | collective-permute-start | bytes 196616 | tf_op jit(solution)/shard_map/ppermute | solution.py:544
  111.3 5.8 %collective-permute-start.21 = (bf16[32,1024]{1,0:T(8,128)(2,1)S(1)}, bf16[32,1024]{1,0:T(8,128)(2,1)S(1)}, u32[]{:S(2)}, u32[]{:S(2)}) collective-permute-start(bf16[32,1024]{1,0:T(8,128)(2,1)S(1)} %get-tuple-element.70), channel_id=1, source_target_pairs={{0,6},{1,7},{2,0},{3,1},{4,2},{5,3},{6,4},{7,5},{8,14},{9,15},{10,... | collective-permute-start | bytes 196616 | tf_op jit(solution)/shard_map/ppermute | solution.py:544
  117.1 8.8 %collective-permute-start.24 = (bf16[32,1024]{1,0:T(8,128)(2,1)S(1)}, bf16[32,1024]{1,0:T(8,128)(2,1)S(1)}, u32[]{:S(2)}, u32[]{:S(2)}) collective-permute-start(bf16[32,1024]{1,0:T(8,128)(2,1)S(1)} %chip_sum.1.refs_13_.refs_0_), channel_id=1, source_target_pairs={{0,6},{1,7},{2,0},{3,1},{4,2},{5,3},{6,4},{7,5},{8,14},{9,15},{10,... | collective-permute-start | bytes 196616 | tf_op jit(solution)/shard_map/ppermute | solution.py:544
  119.5 7.6 %collective-permute-start.23 = (bf16[32,1024]{1,0:T(8,128)(2,1)S(1)}, bf16[32,1024]{1,0:T(8,128)(2,1)S(1)}, u32[]{:S(2)}, u32[]{:S(2)}) collective-permute-start(bf16[32,1024]{1,0:T(8,128)(2,1)S(1)} %chip_sum.1.refs_13_.refs_0_), channel_id=1, source_target_pairs={{0,4},{1,5},{2,6},{3,7},{4,0},{5,1},{6,2},{7,3},{8,12},{9,13},{10,... | collective-permute-start | bytes 196616 | tf_op jit(solution)/shard_map/ppermute | solution.py:544
  120.4 6.8 %collective-permute-start.22 = (bf16[32,1024]{1,0:T(8,128)(2,1)S(1)}, bf16[32,1024]{1,0:T(8,128)(2,1)S(1)}, u32[]{:S(2)}, u32[]{:S(2)}) collective-permute-start(bf16[32,1024]{1,0:T(8,128)(2,1)S(1)} %chip_sum.1.refs_13_.refs_0_), channel_id=1, source_target_pairs={{0,2},{1,3},{2,4},{3,5},{4,6},{5,7},{6,0},{7,1},{8,10},{9,11},{10,... | collective-permute-start | bytes 196616 | tf_op jit(solution)/shard_map/ppermute | solution.py:544
  (21 other events, 164.4 us)

commit v2 on v0

--- a/solution.py
+++ b/solution.py
@@ -72,9 +72,13 @@
     else:
         top, bottom, top_cot, bottom_cot = [refs.pop(0)[...] for _ in range(4)]
         rows = top.shape[0]
-    gain_a_ref, gain_f_ref, down_ref, up_ref = refs[:4]
-    bottom_ref_out, z_ref, up_msg_ref, down_msg_ref, own_ref = refs[4:9]
-    next_ref, na_ref, dhid_ref, hid_ref = refs[9:]
+    gain_a_ref, gain_f_ref, down_ref, up_ref = [refs.pop(0) for _ in range(4)]
+    earlier = [refs.pop(0) for _ in range(4)] if packed else None
+    bottom_ref_out, z_ref, up_msg_ref, down_msg_ref, own_ref = refs[:5]
+    if packed:
+        keep_ref, send_ref, both = refs[5:]
+    else:
+        next_ref, na_ref, dhid_ref, hid_ref = refs[5:]
     columns = down_ref.shape[1]
     first = lax.axis_index("tok") * (rows // BLOCK)
     shape = (rows, columns)
@@ -102,14 +106,22 @@
     up_msg_ref[rows:] = z[rows - WIN :]
     down_msg_ref[:rows] = nf
     down_msg_ref[rows:] = z[:WIN]
-    next_ref[:rows] = bottom.astype(jnp.bfloat16)
-    next_ref[rows:] = z
-    na_ref[...] = na
-    dhid_ref[...] = dhid
-    hid_ref[...] = hid
-
-
-def adapter(packed, blocks, streams, gain_a, gain_f, down, up):
+    if packed:
+        na_one, dhid_one, hid_one, cot_one = [ref[...] for ref in earlier]
+        core = lax.rem(lax.axis_index("tok"), 2)
+        both[0] = contract_first(dhid_one, na_one) + contract_first(dhid, na)
+        both[1] = contract_first(hid_one, cot_one) + contract_first(hid, bottom_cot)
+        keep_ref[...] = both[core]
+        send_ref[...] = both[1 - core].astype(jnp.bfloat16)
+    else:
+        next_ref[:rows] = bottom.astype(jnp.bfloat16)
+        next_ref[rows:] = z
+        na_ref[...] = na
+        dhid_ref[...] = dhid
+        hid_ref[...] = hid
+
+
+def adapter(packed, blocks, streams, gain_a, gain_f, down, up, earlier=()):
     width, columns = down.shape
     rows = streams[0].shape[0] // (2 if packed else 1)
     bf = jnp.bfloat16
@@ -120,54 +132,24 @@
         shape((rows + WIN, width), bf),
         shape((rows + WIN, width), bf),
         shape((2 * rows, width), bf),
-        shape((2 * rows, width), bf),
-        shape((rows, width), bf),
-        shape((rows, columns), bf),
-        shape((rows, columns), bf),
-    )
+    )
+    if packed:
+        outs += (shape((columns, width), jnp.float32), shape((columns, width), bf))
+    else:
+        outs += (shape((2 * rows, width), bf), shape((rows, width), bf))
+        outs += (shape((rows, columns), bf),) * 2
     return pl.pallas_call(
         functools.partial(adapter_kernel, packed),
         out_shape=outs,
-        in_specs=[SMEM_SPEC] + [VMEM_SPEC] * (len(streams) + 4),
+        in_specs=[SMEM_SPEC] + [VMEM_SPEC] * (len(streams) + 4 + len(earlier)),
         out_specs=(VMEM_SPEC,) * len(outs),
+        scratch_shapes=[pltpu.VMEM((2, columns, width), jnp.float32)] if packed else [],
         compiler_params=pltpu.CompilerParams(vmem_limit_bytes=SMALL),
         cost_estimate=pl.CostEstimate(
             flops=8 * rows * width * columns, bytes_accessed=20 * rows * width, transcendentals=0
         ),
         name="adapter",
-    )(blocks, *streams, gain_a, gain_f, down, up)
-
-
-def grads_kernel(
-    na_a, na_b, dhid_a, dhid_b, hid_a, hid_b, cot_a, late_ref, keep_ref, send_ref, both
-):
-    rows, columns = dhid_a.shape
-    core = lax.rem(lax.axis_index("tok"), 2)
-    cot_b = late_ref[rows:]
-    both[0] = contract_first(dhid_a[...], na_a[...]) + contract_first(dhid_b[...], na_b[...])
-    both[1] = contract_first(hid_a[...], cot_a[...]) + contract_first(hid_b[...], cot_b)
-    keep_ref[...] = both[core]
-    send_ref[...] = both[1 - core].astype(jnp.bfloat16)
-
-
-def adapter_grads(*arrays):
-    rows, width = arrays[0].shape
-    columns = arrays[2].shape[1]
-    return pl.pallas_call(
-        grads_kernel,
-        out_shape=(
-            jax.ShapeDtypeStruct((columns, width), jnp.float32),
-            jax.ShapeDtypeStruct((columns, width), jnp.bfloat16),
-        ),
-        in_specs=[VMEM_SPEC] * 8,
-        out_specs=(VMEM_SPEC,) * 2,
-        scratch_shapes=[pltpu.VMEM((2, columns, width), jnp.float32)],
-        compiler_params=pltpu.CompilerParams(vmem_limit_bytes=SMALL),
-        cost_estimate=pl.CostEstimate(
-            flops=8 * rows * width * columns, bytes_accessed=10 * rows * width, transcendentals=0
-        ),
-        name="adapter_grads",
-    )(*arrays)
+    )(blocks, *streams, gain_a, gain_f, down, up, *earlier)
 
 
 def core_sum_kernel(keep_ref, came_ref, out_ref, *send_refs):
@@ -368,10 +350,48 @@
     )(*shards)
 
 
+def distances_kernel(order_ref, logs):
+    queries, keys = logs.shape
+    rows = keys // 3
+    total = order_ref.shape[1] * BLOCK
+    start = lax.axis_index("tok") * rows
+    first = lax.axis_index("tok") * (rows // BLOCK)
+    here = rows // BLOCK
+    reach = WIN // BLOCK
+
+    def places(shape, dim, lead, tail):
+        at = lax.broadcasted_iota(jnp.int32, shape, dim)
+        own_and_after = per_block(order_ref, 1, first, here + lead, shape, dim)
+        skip = here + lead
+        ahead = per_block(order_ref, 1, first - tail - skip, skip + tail, shape, dim)
+        is_before = at >= rows + lead * BLOCK
+        place = jnp.where(is_before, ahead, own_and_after)
+        token = jnp.where(is_before, at - rows - (lead + tail) * BLOCK, at) + start
+        return place, token
+
+    query_place, query_token = places((queries, 1), 0, reach, reach)
+    key_place, key_token = places((1, keys), 1, here, here)
+    near = jnp.abs(query_token - key_token) <= WIN
+    allowed = near & (key_token >= 0) & (key_token < total)
+    gap = jnp.abs(query_place - key_place).astype(jnp.float32)
+    logs[...] = jnp.where(allowed, jnp.log(1.0 + gap), -1.0)
+
+
+def distances(blocks, rows):
+    return pl.pallas_call(
+        distances_kernel,
+        out_shape=jax.ShapeDtypeStruct((rows + 2 * WIN, 3 * rows), jnp.float32),
+        in_specs=[SMEM_SPEC],
+        out_specs=VMEM_SPEC,
+        compiler_params=pltpu.CompilerParams(vmem_limit_bytes=SMALL),
+        name="distances",
+    )(blocks)
+
+
 def attention_kernel(pairs, first_pair, is_first, ends, waits, *refs):
     refs = list(refs)
     take = lambda count: [refs.pop(0) for _ in range(count)]
-    order_ref, scale_ref, slope_ref, own_ref, before_ref, after_ref, w_ref, wo_ref = take(8)
+    scale_ref, slope_ref, logs, own_ref, before_ref, after_ref, w_ref, wo_ref = take(8)
     partial_refs = [] if is_first else take(2)
     if ends == "one":
         top_ref, bottom_ref, bottom_cot_ref, gain_ref = take(4)
@@ -384,13 +404,12 @@
     else:
         take(waits)
         top_part_ref, nf_part_ref, done_ref = take(3)
-    nf_all, z_all, logs, top_acc, nf_acc = refs
+    nf_all, z_all, top_acc, nf_acc = refs
 
     rows, width = top_acc.shape
     head_size = width // scale_ref.shape[1]
     pair = GROUP * head_size
     wide = 3 * pair
-    queries, keys = rows + 2 * WIN, 3 * rows
     nf_all[:rows] = own_ref[:rows]
     nf_all[rows : 2 * rows] = after_ref[:rows]
     nf_all[2 * rows :] = before_ref[:rows]
@@ -403,29 +422,6 @@
     else:
         top_acc[...] = partial_refs[0][...]
         nf_acc[...] = partial_refs[1][...]
-    total = order_ref.shape[1] * BLOCK
-    start = lax.axis_index("tok") * rows
-    first = lax.axis_index("tok") * (rows // BLOCK)
-    here = rows // BLOCK
-    reach = WIN // BLOCK
-
-    def places(shape, dim, lead, tail):
-        at = lax.broadcasted_iota(jnp.int32, shape, dim)
-        own_and_after = per_block(order_ref, 1, first, here + lead, shape, dim)
-        skip = here + lead
-        ahead = per_block(order_ref, 1, first - tail - skip, skip + tail, shape, dim)
-        is_before = at >= rows + lead * BLOCK
-        place = jnp.where(is_before, ahead, own_and_after)
-        token = jnp.where(is_before, at - rows - (lead + tail) * BLOCK, at) + start
-        return place, token
-
-    query_place, query_token = places((queries, 1), 0, reach, reach)
-    key_place, key_token = places((1, keys), 1, here, here)
-    near = jnp.abs(query_token - key_token) <= WIN
-    allowed = near & (key_token >= 0) & (key_token < total)
-    gap = jnp.abs(query_place - key_place).astype(jnp.float32)
-    logs[...] = jnp.where(allowed, jnp.log(1.0 + gap), -1.0)
-
 
     for step in range(pairs):
         nf = nf_all[...]
@@ -495,7 +491,7 @@
 
 
 def attention(blocks, weight, out_weight, first_pair, pairs, partial, ends, last, after):
-    order, scale, slope, own, before, behind = blocks
+    scale, slope, logs, own, before, behind = blocks
     rows, width = own.shape[0] // 2, own.shape[1]
     bf = jnp.bfloat16
     arrays = list(blocks) + [weight, out_weight] + list(partial or ()) + list(last)
@@ -513,12 +509,11 @@
             attention_kernel, pairs, first_pair, partial is None, ends, len(after)
         ),
         out_shape=outs,
-        in_specs=[SMEM_SPEC] * 3 + [VMEM_SPEC] * (len(arrays) - 3) + [ANY_SPEC] * len(after),
+        in_specs=[SMEM_SPEC] * 2 + [VMEM_SPEC] * (len(arrays) - 2) + [ANY_SPEC] * len(after),
         out_specs=(VMEM_SPEC,) * len(outs),
         scratch_shapes=[
             pltpu.VMEM((3 * rows, width), bf),
             pltpu.VMEM((rows + 2 * WIN, width), bf),
-            pltpu.VMEM((rows + 2 * WIN, 3 * rows), jnp.float32),
             pltpu.VMEM((rows, width), jnp.float32),
             pltpu.VMEM((rows, width), jnp.float32),
         ],
@@ -594,7 +589,9 @@
         return ordered(shards, [begin] * 4 + [0] * (2 * len(rest)), size)
 
     w_x = gathered(x_up + x_down[:0:-1], 0, x_size)
-    head_args = (blocks, logit_scale, distance_slope, own, before, behind)
+    rows = own.shape[0] // 2
+    logs_one, logs_two = distances(blocks, rows), distances(next_blocks, rows)
+    head_args = (logit_scale, distance_slope, logs_one, own, before, behind)
     *part, done = attention(
         head_args, w_x, w_x, 0, half, None, None, (), (y_down[-1],)
     )
@@ -604,15 +601,13 @@
     (late,) = attention(head_args, w_y, w_x, half, groups - half, part, "one", last, ())
     late = shifted(late, "section", -1)
 
-    two = adapter(True, next_blocks, (late, early), *params)
-    bottom_two, z_two, up_msg, down_msg, own, _, na_two, dhid_two, hid_two = two
+    earlier = (na_one, dhid_one, hid_one, grad_two[0])
+    two = adapter(True, next_blocks, (late, early), *params, earlier)
+    bottom_two, z_two, up_msg, down_msg, own, keep, send = two
     before, behind = shifted(up_msg, "tok", 1), shifted(down_msg, "tok", -1)
-    keep, send = adapter_grads(
-        na_one, na_two, dhid_one, dhid_two, hid_one, hid_two, grad_two[0], late
-    )
     parts, *sends = core_sum(keep, swapped(send), chips)
     came = [rotated(block, hops) for hops, block in enumerate(sends, 1)]
-    head_args = (next_blocks, logit_scale, distance_slope, own, before, behind)
+    head_args = (logit_scale, distance_slope, logs_two, own, before, behind)
     *part, done = attention(head_args, w_x, w_x, 0, half, None, None, (), (parts,))
     block = chip_sum(parts, came, done)
     blocks_all = [block] + [rotated(block, hops) for hops in range(1, chips)]

time: 130 us -> 130 us (level)
  waiting for transfers between devices: 60.1 us -> 57.5 us
    ppermute x11, waiting for transfers between devices: 44.7 us -> 43.2 us  [rotated(): return lax.ppermute(values, 'tok', pairs)]
  transfers between devices with their start and end apart: 26 -> 26, of which waited for: 11 -> 12; matrix products, arithmetic and copies ran while one was open for 1% -> 1% of each run, Pallas kernels for 12% -> 13%
where the time goes in v2:
time: 130 us; the launch traced here: 129 us
  waiting for transfers between devices  57.5 us (44%)
  starting transfers between devices  34.3 us (26%)
  Pallas kernels  26.9 us (21%)
  local copies, waits for them, and re-layouts  8.26 us (6%)
    ppermute x11, waiting for transfers between devices, rotated(): return lax.ppermute(values, 'tok', pairs)  43.2 us
    ppermute x11, starting transfers between devices, rotated(): return lax.ppermute(values, 'tok', pairs)  19.7 us
    pallas_call x4, Pallas kernels, attention(): pl.pallas_call(functools.partial(attention_kernel, pairs, first_pair, par...  16.6 us
    ppermute x7, waiting for transfers between devices, shifted(): return lax.ppermute(values, axis, pairs)  11.4 us
    ppermute x7, starting transfers between devices, shifted(): return lax.ppermute(values, axis, pairs)  10.3 us
    unnamed x38, local copies, waits for them, and re-layouts  8.26 us
    pallas_call x2, Pallas kernels, adapter(): pl.pallas_call(functools.partial(adapter_kernel, packed), out_shape=outs,...  4.59 us
    ppermute x8, starting transfers between devices, swapped(): return lax.ppermute(values, 'tok', [(i, i ^ 1) for i in range(devices)])  4.29 us
  transfers between devices with their start and end apart: 26, of which 12 were waited for; matrix products, arithmetic and copies ran while one was open for 1% of the time, Pallas kernels for 13%

profile of v2, /device:TPU:0, one launch (start us, length us, event | category | flops | bytes accessed | tf_op | source)
XLA Modules:
  0.0 128.7 jit_solution(9912037741673235819)
XLA Ops:
  0.6 2.6 %arrange.1 = (bf16[128,4096]{1,0:T(8,128)(2,1)}, bf16[128,2560]{1,0:T(8,128)(2,1)}, bf16[128,1536]{1,0:T(8,128)(2,1)}) custom-call(bf16[128,3072]{1,0:T(8,128)(2,1)} %bitcast.26, bf16[128,1024]{1,0:T(8,128)(2,1)} %bitcast.27), custom_call_target="tpu_custom_call" | custom-call | tf_op jit(solution)/shard_map/arrange/pallas_call | solution.py:278
  3.3 3.1 %collective-permute-start.4 = (bf16[128,4096]{1,0:T(8,128)(2,1)}, bf16[128,4096]{1,0:T(8,128)(2,1)S(1)}, u32[]{:S(2)}, u32[]{:S(2)}) collective-permute-start(bf16[128,4096]{1,0:T(8,128)(2,1)} %get-tuple-element.42.values_ref.refs_0_), channel_id=1, source_target_pairs={{0,2},{1,3},{2,4},{3,5},{4,6},{5,7},{6,0},{7,1},{8,10},{9,11},{10,... | collective-permute-start | bytes 3145736 | tf_op jit(solution)/shard_map/ppermute | solution.py:539
  14.0 2.2 %adapter.2 = (f32[64,1024]{1,0:T(8,128)S(1)}, bf16[64,1024]{1,0:T(8,128)(2,1)}, bf16[96,1024]{1,0:T(8,128)(2,1)S(1)}, bf16[96,1024]{1,0:T(8,128)(2,1)S(1)}, bf16...) custom-call(s32[2,32]{1,0:T(2,128)S(1)} %pad_add_fusion.order_ref.re, ...), custom_call_target="tpu_custom_call" | custom-call | flops 67108864 | bytes 1310720 | tf_op jit(solution)/shard_map/adapter/pallas_call | solution.py:141
  19.0 5.0 %collective-permute-start.5 = (bf16[128,1536]{1,0:T(8,128)(2,1)}, bf16[128,1536]{1,0:T(8,128)(2,1)S(1)}, u32[]{:S(2)}, u32[]{:S(2)}) collective-permute-start(bf16[128,1536]{1,0:T(8,128)(2,1)} %get-tuple-element.43), channel_id=1, source_target_pairs={{0,6},{1,7},{2,0},{3,1},{4,2},{5,3},{6,4},{7,5},{8,14},{9,15},{10,... | collective-permute-start | bytes 1179656 | tf_op jit(solution)/shard_map/ppermute | solution.py:539
  24.0 1.9 %collective-permute-start.10 = (bf16[128,2560]{1,0:T(8,128)(2,1)}, bf16[128,2560]{1,0:T(8,128)(2,1)S(1)}, u32[]{:S(2)}, u32[]{:S(2)}) collective-permute-start(bf16[128,2560]{1,0:T(8,128)(2,1)} %get-tuple-element.44), channel_id=1, source_target_pairs={{0,6},{1,7},{2,0},{3,1},{4,2},{5,3},{6,4},{7,5},{8,14},{9,15},{10,... | collective-permute-start | bytes 1966088 | tf_op jit(solution)/shard_map/ppermute | solution.py:539
  25.9 6.7 %collective-permute-done.4.values_ref.refs_2_ = bf16[128,4096]{1,0:T(8,128)(2,1)S(1)} collective-permute-done((bf16[128,4096]{1,0:T(8,128)(2,1)}, bf16[128,4096]{1,0:T(8,128)(2,1)S(1)}, u32[]{:S(2)}, u32[]{:S(2)}) %collective-permute-start.4) | collective-permute-done | bytes 1048608 | tf_op jit(solution)/shard_map/ppermute | solution.py:539
  34.0 3.1 %collective-permute-start.3 = (bf16[128,4096]{1,0:T(8,128)(2,1)S(1)}, bf16[128,4096]{1,0:T(8,128)(2,1)S(1)}, u32[]{:S(2)}, u32[]{:S(2)}) collective-permute-start(bf16[128,4096]{1,0:T(8,128)(2,1)S(1)} %part_of.4), channel_id=1, source_target_pairs={{0,1},{1,0},{2,3},{3,2},{4,5},{5,4},{6,7},{7,6},{8,9},{9,8},{10,11... | collective-permute-start | bytes 3145736 | tf_op jit(solution)/shard_map/ppermute | solution.py:544
  37.2 7.2 %collective-permute-done.5.refs_0_.refs_8_.refs_6_ = bf16[128,1536]{1,0:T(8,128)(2,1)S(1)} collective-permute-done((bf16[128,1536]{1,0:T(8,128)(2,1)}, bf16[128,1536]{1,0:T(8,128)(2,1)S(1)}, u32[]{:S(2)}, u32[]{:S(2)}) %collective-permute-start.5) | collective-permute-done | bytes 393248 | tf_op jit(solution)/shard_map/ppermute | solution.py:539
  44.5 14.7 %collective-permute-done.10.refs_6_ = bf16[128,2560]{1,0:T(8,128)(2,1)S(1)} collective-permute-done((bf16[128,2560]{1,0:T(8,128)(2,1)}, bf16[128,2560]{1,0:T(8,128)(2,1)S(1)}, u32[]{:S(2)}, u32[]{:S(2)}) %collective-permute-start.10) | collective-permute-done | bytes 655392 | tf_op jit(solution)/shard_map/ppermute | solution.py:539
  59.2 11.2 %collective-permute-done.8.refs_4_ = bf16[128,2560]{1,0:T(8,128)(2,1)S(1)} collective-permute-done((bf16[128,2560]{1,0:T(8,128)(2,1)S(1)}, bf16[128,2560]{1,0:T(8,128)(2,1)S(1)}, u32[]{:S(2)}, u32[]{:S(2)}) %collective-permute-start.8) | collective-permute-done | bytes 655392 | tf_op jit(solution)/shard_map/ppermute | solution.py:539
  74.8 3.9 %attention.4 = (f32[64,1024]{1,0:T(8,128)S(1)}, f32[64,1024]{1,0:T(8,128)S(1)}, f32[8,128]{1,0:T(8,128)S(1)}) custom-call(f32[1,8]{1,0:T(1,128)S(1)} %copy-done.17, f32[1,8]{1,0:T(1,128)S(1)} %copy-done.18, f32[128,192]{1,0:T(8,128)S(1)} %distances.3.refs_2_, bf16[128,1024]{1,0:T(8,128)(2,1)S(1)} %get-tuple-element.39.refs_0_.refs_1_.refs_3_, ...), custom_call_target="tpu_custom_call" | custom-call | flops 536870912 | bytes 2097152 | tf_op jit(solution)/shard_map/attention/pallas_call | solution.py:507
  78.7 2.5 %collective-permute-done.order_ref.refs_3_.refs_0_ = s32[2,32]{1,0:T(2,128)S(1)} collective-permute-done((s32[2,32]{1,0:T(2,128)S(1)}, s32[2,32]{1,0:T(2,128)S(1)}, u32[]{:S(2)}, u32[]{:S(2)}) %collective-permute-start) | collective-permute-done | bytes 288 | tf_op jit(solution)/shard_map/ppermute | solution.py:533
  81.2 2.6 %collective-permute-done.7.refs_0_ = bf16[128,1536]{1,0:T(8,128)(2,1)S(1)} collective-permute-done((bf16[128,1536]{1,0:T(8,128)(2,1)S(1)}, bf16[128,1536]{1,0:T(8,128)(2,1)S(1)}, u32[]{:S(2)}, u32[]{:S(2)}) %collective-permute-start.7) | collective-permute-done | bytes 393248 | tf_op jit(solution)/shard_map/ppermute | solution.py:539
  83.8 1.7 %collective-permute-done.13.refs_5_ = bf16[128,1536]{1,0:T(8,128)(2,1)S(1)} collective-permute-done((bf16[128,1536]{1,0:T(8,128)(2,1)S(1)}, bf16[128,1536]{1,0:T(8,128)(2,1)S(1)}, u32[]{:S(2)}, u32[]{:S(2)}) %collective-permute-start.13) | collective-permute-done | bytes 393248 | tf_op jit(solution)/shard_map/ppermute | solution.py:544
  85.8 4.1 %attention.5 = bf16[128,1024]{1,0:T(8,128)(2,1)S(1)} custom-call(f32[1,8]{1,0:T(1,128)S(1)} %copy-done.17, f32[1,8]{1,0:T(1,128)S(1)} %copy-done.18, f32[128,192]{1,0:T(8,128)S(1)} %distances.3.refs_2_, bf16[128,1024]{1,0:T(8,128)(2,1)S(1)} %get-tuple-element.39.refs_0_.refs_1_.refs_3_, bf16[96,1024]{1,0:T(8,128)(2,1)S(1)} %collective-permute-done.1.refs_0_.refs_4_, ...), custom_call_target="tpu_custom_call" | custom-call | flops 536870912 | bytes 2097152 | tf_op jit(solution)/shard_map/attention/pallas_call | solution.py:507
  91.2 8.9 %collective-permute-done.15.refs_1_.refs_10_ = bf16[128,1024]{1,0:T(8,128)(2,1)S(1)} collective-permute-done((bf16[128,1024]{1,0:T(8,128)(2,1)S(1)}, bf16[128,1024]{1,0:T(8,128)(2,1)S(1)}, u32[]{:S(2)}, u32[]{:S(2)}) %collective-permute-start.15) | collective-permute-done | bytes 262176 | tf_op jit(solution)/shard_map/ppermute | solution.py:533
  100.2 2.4 %adapter.3 = (f32[64,1024]{1,0:T(8,128)}, bf16[64,1024]{1,0:T(8,128)(2,1)}, bf16[96,1024]{1,0:T(8,128)(2,1)S(1)}, bf16[96,1024]{1,0:T(8,128)(2,1)S(1)}, bf16[128...) custom-call(s32[2,32]{1,0:T(2,128)S(1)} %collective-permute-done.order_ref.refs_3_.refs_0_, ...), custom_call_target="tpu_custom_call" | custom-call | flops 67108864 | bytes 1310720 | tf_op jit(solution)/shard_map/adapter/pallas_call | solution.py:141
  102.5 2.4 %collective-permute-start.16 = (bf16[96,1024]{1,0:T(8,128)(2,1)S(1)}, bf16[96,1024]{1,0:T(8,128)(2,1)S(1)}, u32[]{:S(2)}, u32[]{:S(2)}) collective-permute-start(bf16[96,1024]{1,0:T(8,128)(2,1)S(1)} %get-tuple-element.54), channel_id=1, source_target_pairs={{0,1},{1,2},{2,3},{3,4},{4,5},{5,6},{6,7},{8,9},{9,10},{10,11},{11... | collective-permute-start | bytes 589832 | tf_op jit(solution)/shard_map/ppermute | solution.py:533
  106.3 2.3 %collective-permute-start.19 = (bf16[32,1024]{1,0:T(8,128)(2,1)S(1)}, bf16[32,1024]{1,0:T(8,128)(2,1)S(1)}, u32[]{:S(2)}, u32[]{:S(2)}) collective-permute-start(bf16[32,1024]{1,0:T(8,128)(2,1)S(1)} %get-tuple-element.62), channel_id=1, source_target_pairs={{0,2},{1,3},{2,4},{3,5},{4,6},{5,7},{6,0},{7,1},{8,10},{9,11},{10,... | collective-permute-start | bytes 196616 | tf_op jit(solution)/shard_map/ppermute | solution.py:539
  108.6 1.8 %collective-permute-start.20 = (bf16[32,1024]{1,0:T(8,128)(2,1)S(1)}, bf16[32,1024]{1,0:T(8,128)(2,1)S(1)}, u32[]{:S(2)}, u32[]{:S(2)}) collective-permute-start(bf16[32,1024]{1,0:T(8,128)(2,1)S(1)} %get-tuple-element.63), channel_id=1, source_target_pairs={{0,4},{1,5},{2,6},{3,7},{4,0},{5,1},{6,2},{7,3},{8,12},{9,13},{10,... | collective-permute-start | bytes 196616 | tf_op jit(solution)/shard_map/ppermute | solution.py:539
  111.9 3.9 %attention.6 = (f32[64,1024]{1,0:T(8,128)S(1)}, f32[64,1024]{1,0:T(8,128)S(1)}, f32[8,128]{1,0:T(8,128)S(1)}) custom-call(f32[1,8]{1,0:T(1,128)S(1)} %copy-done.17, f32[1,8]{1,0:T(1,128)S(1)} %copy-done.18, f32[128,192]{1,0:T(8,128)S(1)} %distances.2.refs_2_, bf16[128,1024]{1,0:T(8,128)(2,1)S(1)} %get-tuple-element.53.refs_3_, ...), custom_call_target="tpu_custom_call" | custom-call | flops 536870912 | bytes 2097152 | tf_op jit(solution)/shard_map/attention/pallas_call | solution.py:507
  116.4 1.7 %collective-permute-start.22 = (bf16[32,1024]{1,0:T(8,128)(2,1)S(1)}, bf16[32,1024]{1,0:T(8,128)(2,1)S(1)}, u32[]{:S(2)}, u32[]{:S(2)}) collective-permute-start(bf16[32,1024]{1,0:T(8,128)(2,1)S(1)} %chip_sum.1.refs_13_.refs_0_), channel_id=1, source_target_pairs={{0,2},{1,3},{2,4},{3,5},{4,6},{5,7},{6,0},{7,1},{8,10},{9,11},{10,... | collective-permute-start | bytes 196616 | tf_op jit(solution)/shard_map/ppermute | solution.py:539
  118.9 2.2 %collective-permute-start.24 = (bf16[32,1024]{1,0:T(8,128)(2,1)S(1)}, bf16[32,1024]{1,0:T(8,128)(2,1)S(1)}, u32[]{:S(2)}, u32[]{:S(2)}) collective-permute-start(bf16[32,1024]{1,0:T(8,128)(2,1)S(1)} %chip_sum.1.refs_13_.refs_0_), channel_id=1, source_target_pairs={{0,6},{1,7},{2,0},{3,1},{4,2},{5,3},{6,4},{7,5},{8,14},{9,15},{10,... | collective-permute-start | bytes 196616 | tf_op jit(solution)/shard_map/ppermute | solution.py:539
  121.1 4.7 %attention.7 = (f32[64,1024]{1,0:T(8,128)}, bf16[64,1024]{1,0:T(8,128)(2,1)}, f32[8,128]{1,0:T(8,128)S(1)}) custom-call(f32[1,8]{1,0:T(1,128)S(1)} %copy-done.17, f32[1,8]{1,0:T(1,128)S(1)} %copy-done.18, f32[128,192]{1,0:T(8,128)S(1)} %distances.2.refs_2_, bf16[128,1024]{1,0:T(8,128)(2,1)S(1)} %get-tuple-element.53.refs_3_, ...), custom_call_target="tpu_custom_call" | custom-call | flops 536870912 | bytes 2097152 | tf_op jit(solution)/shard_map/attention/pallas_call | solution.py:507
  (87 shorter events, 24.9 us)
Async XLA Ops:
  3.3 29.4 %collective-permute-start.4 = (bf16[128,4096]{1,0:T(8,128)(2,1)}, bf16[128,4096]{1,0:T(8,128)(2,1)S(1)}, u32[]{:S(2)}, u32[]{:S(2)}) collective-permute-start(bf16[128,4096]{1,0:T(8,128)(2,1)} %get-tuple-element.42.values_ref.refs_0_), channel_id=1, source_target_pairs={{0,2},{1,3},{2,4},{3,5},{4,6},{5,7},{6,0},{7,1},{8,10},{9,11},{10,... | collective-permute-start | bytes 3145736 | tf_op jit(solution)/shard_map/ppermute | solution.py:539
  16.2 16.5 %collective-permute-start.1 = (bf16[96,1024]{1,0:T(8,128)(2,1)S(1)}, bf16[96,1024]{1,0:T(8,128)(2,1)S(1)}, u32[]{:S(2)}, u32[]{:S(2)}) collective-permute-start(bf16[96,1024]{1,0:T(8,128)(2,1)S(1)} %get-tuple-element.40), channel_id=1, source_target_pairs={{0,1},{1,2},{2,3},{3,4},{4,5},{5,6},{6,7},{8,9},{9,10},{10,11},{11... | collective-permute-start | bytes 589832 | tf_op jit(solution)/shard_map/ppermute | solution.py:533
  17.7 15.0 %collective-permute-start.2 = (bf16[96,1024]{1,0:T(8,128)(2,1)S(1)}, bf16[96,1024]{1,0:T(8,128)(2,1)S(1)}, u32[]{:S(2)}, u32[]{:S(2)}) collective-permute-start(bf16[96,1024]{1,0:T(8,128)(2,1)S(1)} %get-tuple-element.41), channel_id=1, source_target_pairs={{1,0},{2,1},{3,2},{4,3},{5,4},{6,5},{7,6},{9,8},{10,9},{11,10},{12... | collective-permute-start | bytes 589832 | tf_op jit(solution)/shard_map/ppermute | solution.py:533
  19.0 25.4 %collective-permute-start.5 = (bf16[128,1536]{1,0:T(8,128)(2,1)}, bf16[128,1536]{1,0:T(8,128)(2,1)S(1)}, u32[]{:S(2)}, u32[]{:S(2)}) collective-permute-start(bf16[128,1536]{1,0:T(8,128)(2,1)} %get-tuple-element.43), channel_id=1, source_target_pairs={{0,6},{1,7},{2,0},{3,1},{4,2},{5,3},{6,4},{7,5},{8,14},{9,15},{10,... | collective-permute-start | bytes 1179656 | tf_op jit(solution)/shard_map/ppermute | solution.py:539
  24.0 35.2 %collective-permute-start.10 = (bf16[128,2560]{1,0:T(8,128)(2,1)}, bf16[128,2560]{1,0:T(8,128)(2,1)S(1)}, u32[]{:S(2)}, u32[]{:S(2)}) collective-permute-start(bf16[128,2560]{1,0:T(8,128)(2,1)} %get-tuple-element.44), channel_id=1, source_target_pairs={{0,6},{1,7},{2,0},{3,1},{4,2},{5,3},{6,4},{7,5},{8,14},{9,15},{10,... | collective-permute-start | bytes 1966088 | tf_op jit(solution)/shard_map/ppermute | solution.py:539
  32.7 37.7 %collective-permute-start.8 = (bf16[128,2560]{1,0:T(8,128)(2,1)S(1)}, bf16[128,2560]{1,0:T(8,128)(2,1)S(1)}, u32[]{:S(2)}, u32[]{:S(2)}) collective-permute-start(bf16[128,2560]{1,0:T(8,128)(2,1)S(1)} %part_of.7), channel_id=1, source_target_pairs={{0,2},{1,3},{2,4},{3,5},{4,6},{5,7},{6,0},{7,1},{8,10},{9,11},{10,... | collective-permute-start | bytes 1966088 | tf_op jit(solution)/shard_map/ppermute | solution.py:539
  34.0 36.5 %collective-permute-start.3 = (bf16[128,4096]{1,0:T(8,128)(2,1)S(1)}, bf16[128,4096]{1,0:T(8,128)(2,1)S(1)}, u32[]{:S(2)}, u32[]{:S(2)}) collective-permute-start(bf16[128,4096]{1,0:T(8,128)(2,1)S(1)} %part_of.4), channel_id=1, source_target_pairs={{0,1},{1,0},{2,3},{3,2},{4,5},{5,4},{6,7},{7,6},{8,9},{9,8},{10,11... | collective-permute-start | bytes 3145736 | tf_op jit(solution)/shard_map/ppermute | solution.py:544
  44.5 29.3 %collective-permute-start.6 = (bf16[128,4096]{1,0:T(8,128)(2,1)S(1)}, bf16[128,4096]{1,0:T(8,128)(2,1)S(1)}, u32[]{:S(2)}, u32[]{:S(2)}) collective-permute-start(bf16[128,4096]{1,0:T(8,128)(2,1)S(1)} %part_of.5), channel_id=1, source_target_pairs={{0,1},{1,0},{2,3},{3,2},{4,5},{5,4},{6,7},{7,6},{8,9},{9,8},{10,11... | collective-permute-start | bytes 3145736 | tf_op jit(solution)/shard_map/ppermute | solution.py:544
  59.2 13.3 %collective-permute-start.11 = (bf16[128,2560]{1,0:T(8,128)(2,1)S(1)}, bf16[128,2560]{1,0:T(8,128)(2,1)S(1)}, u32[]{:S(2)}, u32[]{:S(2)}) collective-permute-start(bf16[128,2560]{1,0:T(8,128)(2,1)S(1)} %collective-permute-done.10.refs_6_), channel_id=1, source_target_pairs={{0,1},{1,0},{2,3},{3,2},{4,5},{5,4},{6,7},{7,6},{8,9},{9,8},{10,11... | collective-permute-start | bytes 1966088 | tf_op jit(solution)/shard_map/ppermute | solution.py:544
  70.4 4.0 %collective-permute-start.9 = (bf16[128,2560]{1,0:T(8,128)(2,1)S(1)}, bf16[128,2560]{1,0:T(8,128)(2,1)S(1)}, u32[]{:S(2)}, u32[]{:S(2)}) collective-permute-start(bf16[128,2560]{1,0:T(8,128)(2,1)S(1)} %collective-permute-done.8.refs_4_), channel_id=1, source_target_pairs={{0,1},{1,0},{2,3},{3,2},{4,5},{5,4},{6,7},{7,6},{8,9},{9,8},{10,11... | collective-permute-start | bytes 1966088 | tf_op jit(solution)/shard_map/ppermute | solution.py:544
  70.4 13.4 %collective-permute-start.7 = (bf16[128,1536]{1,0:T(8,128)(2,1)S(1)}, bf16[128,1536]{1,0:T(8,128)(2,1)S(1)}, u32[]{:S(2)}, u32[]{:S(2)}) collective-permute-start(bf16[128,1536]{1,0:T(8,128)(2,1)S(1)} %part_of.6), channel_id=1, source_target_pairs={{0,2},{1,3},{2,4},{3,5},{4,6},{5,7},{6,0},{7,1},{8,10},{9,11},{10,... | collective-permute-start | bytes 1179656 | tf_op jit(solution)/shard_map/ppermute | solution.py:539
  70.5 10.7 %collective-permute-start.12 = (bf16[128,1024]{1,0:T(8,128)(2,1)S(1)}, bf16[128,1024]{1,0:T(8,128)(2,1)S(1)}, u32[]{:S(2)}, u32[]{:S(2)}) collective-permute-start(bf16[128,1024]{1,0:T(8,128)(2,1)S(1)} %get-tuple-element.46), channel_id=1, source_target_pairs={{8,0},{16,8},{24,16},{9,1},{17,9},{25,17},{10,2},{18,10},{26,18},{... | collective-permute-start | bytes 786440 | tf_op jit(solution)/shard_map/ppermute | solution.py:533
  72.5 8.7 %collective-permute-start = (s32[2,32]{1,0:T(2,128)S(1)}, s32[2,32]{1,0:T(2,128)S(1)}, u32[]{:S(2)}, u32[]{:S(2)}) collective-permute-start(s32[2,32]{1,0:T(2,128)S(1)} %pad_add_fusion.order_ref.refs_0_), channel_id=1, source_target_pairs={{8,0},{16,8},{24,16},{9,1},{17,9},{25,17},{10,2},{18,10},{26,18},{... | collective-permute-start | bytes 776 | tf_op jit(solution)/shard_map/ppermute | solution.py:533
  73.8 10.0 %collective-permute-start.14 = (bf16[128,1536]{1,0:T(8,128)(2,1)S(1)}, bf16[128,1536]{1,0:T(8,128)(2,1)S(1)}, u32[]{:S(2)}, u32[]{:S(2)}) collective-permute-start(bf16[128,1536]{1,0:T(8,128)(2,1)S(1)} %collective-permute-done.5.refs_0_.refs_8_.refs_6_), channel_id=1, source_target_pairs={{0,1},{1,0},{2,3},{3,2},{4,5},{5,4},{6,7},{7,6},{8,9},{9,8},{10,11... | collective-permute-start | bytes 1179656 | tf_op jit(solution)/shard_map/ppermute | solution.py:544
  89.9 10.2 %collective-permute-start.15 = (bf16[128,1024]{1,0:T(8,128)(2,1)S(1)}, bf16[128,1024]{1,0:T(8,128)(2,1)S(1)}, u32[]{:S(2)}, u32[]{:S(2)}) collective-permute-start(bf16[128,1024]{1,0:T(8,128)(2,1)S(1)} %attention.5), channel_id=1, source_target_pairs={{8,0},{16,8},{24,16},{9,1},{17,9},{25,17},{10,2},{18,10},{26,18},{... | collective-permute-start | bytes 786440 | tf_op jit(solution)/shard_map/ppermute | solution.py:533
  102.5 3.7 %collective-permute-start.18 = (bf16[128,1024]{1,0:T(8,128)(2,1)S(1)}, bf16[128,1024]{1,0:T(8,128)(2,1)S(1)}, u32[]{:S(2)}, u32[]{:S(2)}) collective-permute-start(bf16[128,1024]{1,0:T(8,128)(2,1)S(1)} %get-tuple-element.57), channel_id=1, source_target_pairs={{0,1},{1,0},{2,3},{3,2},{4,5},{5,4},{6,7},{7,6},{8,9},{9,8},{10,11... | collective-permute-start | bytes 786440 | tf_op jit(solution)/shard_map/ppermute | solution.py:544
  102.5 9.3 %collective-permute-start.16 = (bf16[96,1024]{1,0:T(8,128)(2,1)S(1)}, bf16[96,1024]{1,0:T(8,128)(2,1)S(1)}, u32[]{:S(2)}, u32[]{:S(2)}) collective-permute-start(bf16[96,1024]{1,0:T(8,128)(2,1)S(1)} %get-tuple-element.54), channel_id=1, source_target_pairs={{0,1},{1,2},{2,3},{3,4},{4,5},{5,6},{6,7},{8,9},{9,10},{10,11},{11... | collective-permute-start | bytes 589832 | tf_op jit(solution)/shard_map/ppermute | solution.py:533
  104.9 6.9 %collective-permute-start.17 = (bf16[96,1024]{1,0:T(8,128)(2,1)S(1)}, bf16[96,1024]{1,0:T(8,128)(2,1)S(1)}, u32[]{:S(2)}, u32[]{:S(2)}) collective-permute-start(bf16[96,1024]{1,0:T(8,128)(2,1)S(1)} %get-tuple-element.55), channel_id=1, source_target_pairs={{1,0},{2,1},{3,2},{4,3},{5,4},{6,5},{7,6},{9,8},{10,9},{11,10},{12... | collective-permute-start | bytes 589832 | tf_op jit(solution)/shard_map/ppermute | solution.py:533
  106.3 9.8 %collective-permute-start.19 = (bf16[32,1024]{1,0:T(8,128)(2,1)S(1)}, bf16[32,1024]{1,0:T(8,128)(2,1)S(1)}, u32[]{:S(2)}, u32[]{:S(2)}) collective-permute-start(bf16[32,1024]{1,0:T(8,128)(2,1)S(1)} %get-tuple-element.62), channel_id=1, source_target_pairs={{0,2},{1,3},{2,4},{3,5},{4,6},{5,7},{6,0},{7,1},{8,10},{9,11},{10,... | collective-permute-start | bytes 196616 | tf_op jit(solution)/shard_map/ppermute | solution.py:539
  108.6 7.5 %collective-permute-start.20 = (bf16[32,1024]{1,0:T(8,128)(2,1)S(1)}, bf16[32,1024]{1,0:T(8,128)(2,1)S(1)}, u32[]{:S(2)}, u32[]{:S(2)}) collective-permute-start(bf16[32,1024]{1,0:T(8,128)(2,1)S(1)} %get-tuple-element.63), channel_id=1, source_target_pairs={{0,4},{1,5},{2,6},{3,7},{4,0},{5,1},{6,2},{7,3},{8,12},{9,13},{10,... | collective-permute-start | bytes 196616 | tf_op jit(solution)/shard_map/ppermute | solution.py:539
  110.4 5.9 %collective-permute-start.21 = (bf16[32,1024]{1,0:T(8,128)(2,1)S(1)}, bf16[32,1024]{1,0:T(8,128)(2,1)S(1)}, u32[]{:S(2)}, u32[]{:S(2)}) collective-permute-start(bf16[32,1024]{1,0:T(8,128)(2,1)S(1)} %get-tuple-element.64), channel_id=1, source_target_pairs={{0,6},{1,7},{2,0},{3,1},{4,2},{5,3},{6,4},{7,5},{8,14},{9,15},{10,... | collective-permute-start | bytes 196616 | tf_op jit(solution)/shard_map/ppermute | solution.py:539
  116.4 9.5 %collective-permute-start.22 = (bf16[32,1024]{1,0:T(8,128)(2,1)S(1)}, bf16[32,1024]{1,0:T(8,128)(2,1)S(1)}, u32[]{:S(2)}, u32[]{:S(2)}) collective-permute-start(bf16[32,1024]{1,0:T(8,128)(2,1)S(1)} %chip_sum.1.refs_13_.refs_0_), channel_id=1, source_target_pairs={{0,2},{1,3},{2,4},{3,5},{4,6},{5,7},{6,0},{7,1},{8,10},{9,11},{10,... | collective-permute-start | bytes 196616 | tf_op jit(solution)/shard_map/ppermute | solution.py:539
  118.1 8.0 %collective-permute-start.23 = (bf16[32,1024]{1,0:T(8,128)(2,1)S(1)}, bf16[32,1024]{1,0:T(8,128)(2,1)S(1)}, u32[]{:S(2)}, u32[]{:S(2)}) collective-permute-start(bf16[32,1024]{1,0:T(8,128)(2,1)S(1)} %chip_sum.1.refs_13_.refs_0_), channel_id=1, source_target_pairs={{0,4},{1,5},{2,6},{3,7},{4,0},{5,1},{6,2},{7,3},{8,12},{9,13},{10,... | collective-permute-start | bytes 196616 | tf_op jit(solution)/shard_map/ppermute | solution.py:539
  118.9 7.1 %collective-permute-start.24 = (bf16[32,1024]{1,0:T(8,128)(2,1)S(1)}, bf16[32,1024]{1,0:T(8,128)(2,1)S(1)}, u32[]{:S(2)}, u32[]{:S(2)}) collective-permute-start(bf16[32,1024]{1,0:T(8,128)(2,1)S(1)} %chip_sum.1.refs_13_.refs_0_), channel_id=1, source_target_pairs={{0,6},{1,7},{2,0},{3,1},{4,2},{5,3},{6,4},{7,5},{8,14},{9,15},{10,... | collective-permute-start | bytes 196616 | tf_op jit(solution)/shard_map/ppermute | solution.py:539
  (21 other events, 160.9 us)

commit v3 on v2

--- a/solution.py
+++ b/solution.py
@@ -61,7 +61,7 @@
     return out
 
 
-def adapter_kernel(packed, *refs):
+def adapter_kernel(packed, waits, *refs):
     refs = list(refs)
     blocks_ref = refs.pop(0)
     if packed:
@@ -74,6 +74,7 @@
         rows = top.shape[0]
     gain_a_ref, gain_f_ref, down_ref, up_ref = [refs.pop(0) for _ in range(4)]
     earlier = [refs.pop(0) for _ in range(4)] if packed else None
+    refs = refs[waits:]
     bottom_ref_out, z_ref, up_msg_ref, down_msg_ref, own_ref = refs[:5]
     if packed:
         keep_ref, send_ref, both = refs[5:]
@@ -121,7 +122,7 @@
         hid_ref[...] = hid
 
 
-def adapter(packed, blocks, streams, gain_a, gain_f, down, up, earlier=()):
+def adapter(packed, blocks, streams, gain_a, gain_f, down, up, earlier=(), after=()):
     width, columns = down.shape
     rows = streams[0].shape[0] // (2 if packed else 1)
     bf = jnp.bfloat16
@@ -139,9 +140,10 @@
         outs += (shape((2 * rows, width), bf), shape((rows, width), bf))
         outs += (shape((rows, columns), bf),) * 2
     return pl.pallas_call(
-        functools.partial(adapter_kernel, packed),
+        functools.partial(adapter_kernel, packed, len(after)),
         out_shape=outs,
-        in_specs=[SMEM_SPEC] + [VMEM_SPEC] * (len(streams) + 4 + len(earlier)),
+        in_specs=[SMEM_SPEC] + [VMEM_SPEC] * (len(streams) + 4 + len(earlier))
+        + [ANY_SPEC] * len(after),
         out_specs=(VMEM_SPEC,) * len(outs),
         scratch_shapes=[pltpu.VMEM((2, columns, width), jnp.float32)] if packed else [],
         compiler_params=pltpu.CompilerParams(vmem_limit_bytes=SMALL),
@@ -149,7 +151,7 @@
             flops=8 * rows * width * columns, bytes_accessed=20 * rows * width, transcendentals=0
         ),
         name="adapter",
-    )(blocks, *streams, gain_a, gain_f, down, up, *earlier)
+    )(blocks, *streams, gain_a, gain_f, down, up, *earlier, *after)
 
 
 def core_sum_kernel(keep_ref, came_ref, out_ref, *send_refs):
@@ -602,7 +604,7 @@
     late = shifted(late, "section", -1)
 
     earlier = (na_one, dhid_one, hid_one, grad_two[0])
-    two = adapter(True, next_blocks, (late, early), *params, earlier)
+    two = adapter(True, next_blocks, (late, early), *params, earlier, (logs_two,))
     bottom_two, z_two, up_msg, down_msg, own, keep, send = two
     before, behind = shifted(up_msg, "tok", 1), shifted(down_msg, "tok", -1)
     parts, *sends = core_sum(keep, swapped(send), chips)

time: 130 us -> 130 us (level)
  no operation moved by 1% of the time
where the time goes in v3:
time: 130 us; the launch traced here: 129 us
  waiting for transfers between devices  57.5 us (44%)
  starting transfers between devices  34.3 us (26%)
  Pallas kernels  27 us (21%)
  local copies, waits for them, and re-layouts  8.25 us (6%)
    ppermute x11, waiting for transfers between devices, rotated(): return lax.ppermute(values, 'tok', pairs)  43.8 us
    ppermute x11, starting transfers between devices, rotated(): return lax.ppermute(values, 'tok', pairs)  19.7 us
    pallas_call x4, Pallas kernels, attention(): pl.pallas_call(functools.partial(attention_kernel, pairs, first_pair, par...  16.6 us
    ppermute x7, waiting for transfers between devices, shifted(): return lax.ppermute(values, axis, pairs)  10.8 us
    ppermute x7, starting transfers between devices, shifted(): return lax.ppermute(values, axis, pairs)  10.3 us
    unnamed x38, local copies, waits for them, and re-layouts  8.25 us
    pallas_call x2, Pallas kernels, adapter(): pl.pallas_call(functools.partial(adapter_kernel, packed, len(after)), out...  4.59 us
    ppermute x8, starting transfers between devices, swapped(): return lax.ppermute(values, 'tok', [(i, i ^ 1) for i in range(devices)])  4.3 us
  transfers between devices with their start and end apart: 26, of which 12 were waited for; matrix products, arithmetic and copies ran while one was open for 1% of the time, Pallas kernels for 13%

profile of v3, /device:TPU:0, one launch (start us, length us, event | category | flops | bytes accessed | tf_op | source)
XLA Modules:
  0.0 128.7 jit_solution(9903021088853318130)
XLA Ops:
  0.6 2.6 %arrange.1 = (bf16[128,4096]{1,0:T(8,128)(2,1)}, bf16[128,2560]{1,0:T(8,128)(2,1)}, bf16[128,1536]{1,0:T(8,128)(2,1)}) custom-call(bf16[128,3072]{1,0:T(8,128)(2,1)} %bitcast.26, bf16[128,1024]{1,0:T(8,128)(2,1)} %bitcast.27), custom_call_target="tpu_custom_call" | custom-call | tf_op jit(solution)/shard_map/arrange/pallas_call | solution.py:280
  3.3 3.1 %collective-permute-start.4 = (bf16[128,4096]{1,0:T(8,128)(2,1)}, bf16[128,4096]{1,0:T(8,128)(2,1)S(1)}, u32[]{:S(2)}, u32[]{:S(2)}) collective-permute-start(bf16[128,4096]{1,0:T(8,128)(2,1)} %get-tuple-element.42.values_ref.refs_0_), channel_id=1, source_target_pairs={{0,2},{1,3},{2,4},{3,5},{4,6},{5,7},{6,0},{7,1},{8,10},{9,11},{10,... | collective-permute-start | bytes 3145736 | tf_op jit(solution)/shard_map/ppermute | solution.py:541
  14.0 2.2 %adapter.2 = (f32[64,1024]{1,0:T(8,128)S(1)}, bf16[64,1024]{1,0:T(8,128)(2,1)}, bf16[96,1024]{1,0:T(8,128)(2,1)S(1)}, bf16[96,1024]{1,0:T(8,128)(2,1)S(1)}, bf16...) custom-call(s32[2,32]{1,0:T(2,128)S(1)} %pad_add_fusion.order_ref.re, ...), custom_call_target="tpu_custom_call" | custom-call | flops 67108864 | bytes 1310720 | tf_op jit(solution)/shard_map/adapter/pallas_call | solution.py:142
  19.0 5.0 %collective-permute-start.5 = (bf16[128,1536]{1,0:T(8,128)(2,1)}, bf16[128,1536]{1,0:T(8,128)(2,1)S(1)}, u32[]{:S(2)}, u32[]{:S(2)}) collective-permute-start(bf16[128,1536]{1,0:T(8,128)(2,1)} %get-tuple-element.43), channel_id=1, source_target_pairs={{0,6},{1,7},{2,0},{3,1},{4,2},{5,3},{6,4},{7,5},{8,14},{9,15},{10,... | collective-permute-start | bytes 1179656 | tf_op jit(solution)/shard_map/ppermute | solution.py:541
  24.0 1.9 %collective-permute-start.10 = (bf16[128,2560]{1,0:T(8,128)(2,1)}, bf16[128,2560]{1,0:T(8,128)(2,1)S(1)}, u32[]{:S(2)}, u32[]{:S(2)}) collective-permute-start(bf16[128,2560]{1,0:T(8,128)(2,1)} %get-tuple-element.44), channel_id=1, source_target_pairs={{0,6},{1,7},{2,0},{3,1},{4,2},{5,3},{6,4},{7,5},{8,14},{9,15},{10,... | collective-permute-start | bytes 1966088 | tf_op jit(solution)/shard_map/ppermute | solution.py:541
  25.9 6.7 %collective-permute-done.4.values_ref.refs_2_ = bf16[128,4096]{1,0:T(8,128)(2,1)S(1)} collective-permute-done((bf16[128,4096]{1,0:T(8,128)(2,1)}, bf16[128,4096]{1,0:T(8,128)(2,1)S(1)}, u32[]{:S(2)}, u32[]{:S(2)}) %collective-permute-start.4) | collective-permute-done | bytes 1048608 | tf_op jit(solution)/shard_map/ppermute | solution.py:541
  34.0 3.1 %collective-permute-start.3 = (bf16[128,4096]{1,0:T(8,128)(2,1)S(1)}, bf16[128,4096]{1,0:T(8,128)(2,1)S(1)}, u32[]{:S(2)}, u32[]{:S(2)}) collective-permute-start(bf16[128,4096]{1,0:T(8,128)(2,1)S(1)} %part_of.4), channel_id=1, source_target_pairs={{0,1},{1,0},{2,3},{3,2},{4,5},{5,4},{6,7},{7,6},{8,9},{9,8},{10,11... | collective-permute-start | bytes 3145736 | tf_op jit(solution)/shard_map/ppermute | solution.py:546
  37.2 7.2 %collective-permute-done.5.refs_0_.refs_8_.refs_6_ = bf16[128,1536]{1,0:T(8,128)(2,1)S(1)} collective-permute-done((bf16[128,1536]{1,0:T(8,128)(2,1)}, bf16[128,1536]{1,0:T(8,128)(2,1)S(1)}, u32[]{:S(2)}, u32[]{:S(2)}) %collective-permute-start.5) | collective-permute-done | bytes 393248 | tf_op jit(solution)/shard_map/ppermute | solution.py:541
  44.5 14.7 %collective-permute-done.10.refs_6_ = bf16[128,2560]{1,0:T(8,128)(2,1)S(1)} collective-permute-done((bf16[128,2560]{1,0:T(8,128)(2,1)}, bf16[128,2560]{1,0:T(8,128)(2,1)S(1)}, u32[]{:S(2)}, u32[]{:S(2)}) %collective-permute-start.10) | collective-permute-done | bytes 655392 | tf_op jit(solution)/shard_map/ppermute | solution.py:541
  59.2 11.2 %collective-permute-done.8.refs_4_ = bf16[128,2560]{1,0:T(8,128)(2,1)S(1)} collective-permute-done((bf16[128,2560]{1,0:T(8,128)(2,1)S(1)}, bf16[128,2560]{1,0:T(8,128)(2,1)S(1)}, u32[]{:S(2)}, u32[]{:S(2)}) %collective-permute-start.8) | collective-permute-done | bytes 655392 | tf_op jit(solution)/shard_map/ppermute | solution.py:541
  74.8 3.9 %attention.4 = (f32[64,1024]{1,0:T(8,128)S(1)}, f32[64,1024]{1,0:T(8,128)S(1)}, f32[8,128]{1,0:T(8,128)S(1)}) custom-call(f32[1,8]{1,0:T(1,128)S(1)} %copy-done.17, f32[1,8]{1,0:T(1,128)S(1)} %copy-done.18, f32[128,192]{1,0:T(8,128)S(1)} %distances.3.refs_2_, bf16[128,1024]{1,0:T(8,128)(2,1)S(1)} %get-tuple-element.39.refs_0_.refs_1_.refs_3_, ...), custom_call_target="tpu_custom_call" | custom-call | flops 536870912 | bytes 2097152 | tf_op jit(solution)/shard_map/attention/pallas_call | solution.py:509
  78.7 2.5 %collective-permute-done.order_ref.refs_3_.refs_0_ = s32[2,32]{1,0:T(2,128)S(1)} collective-permute-done((s32[2,32]{1,0:T(2,128)S(1)}, s32[2,32]{1,0:T(2,128)S(1)}, u32[]{:S(2)}, u32[]{:S(2)}) %collective-permute-start) | collective-permute-done | bytes 288 | tf_op jit(solution)/shard_map/ppermute | solution.py:535
  81.2 2.6 %collective-permute-done.7.refs_0_ = bf16[128,1536]{1,0:T(8,128)(2,1)S(1)} collective-permute-done((bf16[128,1536]{1,0:T(8,128)(2,1)S(1)}, bf16[128,1536]{1,0:T(8,128)(2,1)S(1)}, u32[]{:S(2)}, u32[]{:S(2)}) %collective-permute-start.7) | collective-permute-done | bytes 393248 | tf_op jit(solution)/shard_map/ppermute | solution.py:541
  83.8 1.7 %collective-permute-done.13.refs_5_ = bf16[128,1536]{1,0:T(8,128)(2,1)S(1)} collective-permute-done((bf16[128,1536]{1,0:T(8,128)(2,1)S(1)}, bf16[128,1536]{1,0:T(8,128)(2,1)S(1)}, u32[]{:S(2)}, u32[]{:S(2)}) %collective-permute-start.13) | collective-permute-done | bytes 393248 | tf_op jit(solution)/shard_map/ppermute | solution.py:546
  85.8 4.1 %attention.5 = bf16[128,1024]{1,0:T(8,128)(2,1)S(1)} custom-call(f32[1,8]{1,0:T(1,128)S(1)} %copy-done.17, f32[1,8]{1,0:T(1,128)S(1)} %copy-done.18, f32[128,192]{1,0:T(8,128)S(1)} %distances.3.refs_2_, bf16[128,1024]{1,0:T(8,128)(2,1)S(1)} %get-tuple-element.39.refs_0_.refs_1_.refs_3_, bf16[96,1024]{1,0:T(8,128)(2,1)S(1)} %collective-permute-done.1.refs_0_.refs_4_, ...), custom_call_target="tpu_custom_call" | custom-call | flops 536870912 | bytes 2097152 | tf_op jit(solution)/shard_map/attention/pallas_call | solution.py:509
  91.9 8.3 %collective-permute-done.15.refs_1_.refs_10_ = bf16[128,1024]{1,0:T(8,128)(2,1)S(1)} collective-permute-done((bf16[128,1024]{1,0:T(8,128)(2,1)S(1)}, bf16[128,1024]{1,0:T(8,128)(2,1)S(1)}, u32[]{:S(2)}, u32[]{:S(2)}) %collective-permute-start.15) | collective-permute-done | bytes 262176 | tf_op jit(solution)/shard_map/ppermute | solution.py:535
  100.2 2.4 %adapter.3 = (f32[64,1024]{1,0:T(8,128)}, bf16[64,1024]{1,0:T(8,128)(2,1)}, bf16[96,1024]{1,0:T(8,128)(2,1)S(1)}, bf16[96,1024]{1,0:T(8,128)(2,1)S(1)}, bf16[128...) custom-call(s32[2,32]{1,0:T(2,128)S(1)} %collective-permute-done.order_ref.refs_3_.refs_0_, ...), custom_call_target="tpu_custom_call" | custom-call | flops 67108864 | bytes 1310720 | tf_op jit(solution)/shard_map/adapter/pallas_call | solution.py:142
  102.5 2.4 %collective-permute-start.16 = (bf16[96,1024]{1,0:T(8,128)(2,1)S(1)}, bf16[96,1024]{1,0:T(8,128)(2,1)S(1)}, u32[]{:S(2)}, u32[]{:S(2)}) collective-permute-start(bf16[96,1024]{1,0:T(8,128)(2,1)S(1)} %get-tuple-element.54), channel_id=1, source_target_pairs={{0,1},{1,2},{2,3},{3,4},{4,5},{5,6},{6,7},{8,9},{9,10},{10,11},{11... | collective-permute-start | bytes 589832 | tf_op jit(solution)/shard_map/ppermute | solution.py:535
  106.3 2.3 %collective-permute-start.19 = (bf16[32,1024]{1,0:T(8,128)(2,1)S(1)}, bf16[32,1024]{1,0:T(8,128)(2,1)S(1)}, u32[]{:S(2)}, u32[]{:S(2)}) collective-permute-start(bf16[32,1024]{1,0:T(8,128)(2,1)S(1)} %get-tuple-element.62), channel_id=1, source_target_pairs={{0,2},{1,3},{2,4},{3,5},{4,6},{5,7},{6,0},{7,1},{8,10},{9,11},{10,... | collective-permute-start | bytes 196616 | tf_op jit(solution)/shard_map/ppermute | solution.py:541
  108.6 1.8 %collective-permute-start.20 = (bf16[32,1024]{1,0:T(8,128)(2,1)S(1)}, bf16[32,1024]{1,0:T(8,128)(2,1)S(1)}, u32[]{:S(2)}, u32[]{:S(2)}) collective-permute-start(bf16[32,1024]{1,0:T(8,128)(2,1)S(1)} %get-tuple-element.63), channel_id=1, source_target_pairs={{0,4},{1,5},{2,6},{3,7},{4,0},{5,1},{6,2},{7,3},{8,12},{9,13},{10,... | collective-permute-start | bytes 196616 | tf_op jit(solution)/shard_map/ppermute | solution.py:541
  111.2 3.9 %attention.6 = (f32[64,1024]{1,0:T(8,128)S(1)}, f32[64,1024]{1,0:T(8,128)S(1)}, f32[8,128]{1,0:T(8,128)S(1)}) custom-call(f32[1,8]{1,0:T(1,128)S(1)} %copy-done.17, f32[1,8]{1,0:T(1,128)S(1)} %copy-done.18, f32[128,192]{1,0:T(8,128)S(1)} %distances.2.refs_11_.refs_2_, bf16[128,1024]{1,0:T(8,128)(2,1)S(1)} %get-tuple-element.53.refs_3_, ...), custom_call_target="tpu_custom_call" | custom-call | flops 536870912 | bytes 2097152 | tf_op jit(solution)/shard_map/attention/pallas_call | solution.py:509
  116.4 1.7 %collective-permute-start.22 = (bf16[32,1024]{1,0:T(8,128)(2,1)S(1)}, bf16[32,1024]{1,0:T(8,128)(2,1)S(1)}, u32[]{:S(2)}, u32[]{:S(2)}) collective-permute-start(bf16[32,1024]{1,0:T(8,128)(2,1)S(1)} %chip_sum.1.refs_13_.refs_0_), channel_id=1, source_target_pairs={{0,2},{1,3},{2,4},{3,5},{4,6},{5,7},{6,0},{7,1},{8,10},{9,11},{10,... | collective-permute-start | bytes 196616 | tf_op jit(solution)/shard_map/ppermute | solution.py:541
  118.9 2.2 %collective-permute-start.24 = (bf16[32,1024]{1,0:T(8,128)(2,1)S(1)}, bf16[32,1024]{1,0:T(8,128)(2,1)S(1)}, u32[]{:S(2)}, u32[]{:S(2)}) collective-permute-start(bf16[32,1024]{1,0:T(8,128)(2,1)S(1)} %chip_sum.1.refs_13_.refs_0_), channel_id=1, source_target_pairs={{0,6},{1,7},{2,0},{3,1},{4,2},{5,3},{6,4},{7,5},{8,14},{9,15},{10,... | collective-permute-start | bytes 196616 | tf_op jit(solution)/shard_map/ppermute | solution.py:541
  121.1 4.7 %attention.7 = (f32[64,1024]{1,0:T(8,128)}, bf16[64,1024]{1,0:T(8,128)(2,1)}, f32[8,128]{1,0:T(8,128)S(1)}) custom-call(f32[1,8]{1,0:T(1,128)S(1)} %copy-done.17, f32[1,8]{1,0:T(1,128)S(1)} %copy-done.18, f32[128,192]{1,0:T(8,128)S(1)} %distances.2.refs_11_.refs_2_, bf16[128,1024]{1,0:T(8,128)(2,1)S(1)} %get-tuple-element.53.refs_3_, ...), custom_call_target="tpu_custom_call" | custom-call | flops 536870912 | bytes 2097152 | tf_op jit(solution)/shard_map/attention/pallas_call | solution.py:509
  (87 shorter events, 25.6 us)
Async XLA Ops:
  3.3 29.4 %collective-permute-start.4 = (bf16[128,4096]{1,0:T(8,128)(2,1)}, bf16[128,4096]{1,0:T(8,128)(2,1)S(1)}, u32[]{:S(2)}, u32[]{:S(2)}) collective-permute-start(bf16[128,4096]{1,0:T(8,128)(2,1)} %get-tuple-element.42.values_ref.refs_0_), channel_id=1, source_target_pairs={{0,2},{1,3},{2,4},{3,5},{4,6},{5,7},{6,0},{7,1},{8,10},{9,11},{10,... | collective-permute-start | bytes 3145736 | tf_op jit(solution)/shard_map/ppermute | solution.py:541
  16.2 16.5 %collective-permute-start.1 = (bf16[96,1024]{1,0:T(8,128)(2,1)S(1)}, bf16[96,1024]{1,0:T(8,128)(2,1)S(1)}, u32[]{:S(2)}, u32[]{:S(2)}) collective-permute-start(bf16[96,1024]{1,0:T(8,128)(2,1)S(1)} %get-tuple-element.40), channel_id=1, source_target_pairs={{0,1},{1,2},{2,3},{3,4},{4,5},{5,6},{6,7},{8,9},{9,10},{10,11},{11... | collective-permute-start | bytes 589832 | tf_op jit(solution)/shard_map/ppermute | solution.py:535
  17.7 15.0 %collective-permute-start.2 = (bf16[96,1024]{1,0:T(8,128)(2,1)S(1)}, bf16[96,1024]{1,0:T(8,128)(2,1)S(1)}, u32[]{:S(2)}, u32[]{:S(2)}) collective-permute-start(bf16[96,1024]{1,0:T(8,128)(2,1)S(1)} %get-tuple-element.41), channel_id=1, source_target_pairs={{1,0},{2,1},{3,2},{4,3},{5,4},{6,5},{7,6},{9,8},{10,9},{11,10},{12... | collective-permute-start | bytes 589832 | tf_op jit(solution)/shard_map/ppermute | solution.py:535
  19.0 25.4 %collective-permute-start.5 = (bf16[128,1536]{1,0:T(8,128)(2,1)}, bf16[128,1536]{1,0:T(8,128)(2,1)S(1)}, u32[]{:S(2)}, u32[]{:S(2)}) collective-permute-start(bf16[128,1536]{1,0:T(8,128)(2,1)} %get-tuple-element.43), channel_id=1, source_target_pairs={{0,6},{1,7},{2,0},{3,1},{4,2},{5,3},{6,4},{7,5},{8,14},{9,15},{10,... | collective-permute-start | bytes 1179656 | tf_op jit(solution)/shard_map/ppermute | solution.py:541
  24.0 35.2 %collective-permute-start.10 = (bf16[128,2560]{1,0:T(8,128)(2,1)}, bf16[128,2560]{1,0:T(8,128)(2,1)S(1)}, u32[]{:S(2)}, u32[]{:S(2)}) collective-permute-start(bf16[128,2560]{1,0:T(8,128)(2,1)} %get-tuple-element.44), channel_id=1, source_target_pairs={{0,6},{1,7},{2,0},{3,1},{4,2},{5,3},{6,4},{7,5},{8,14},{9,15},{10,... | collective-permute-start | bytes 1966088 | tf_op jit(solution)/shard_map/ppermute | solution.py:541
  32.7 37.7 %collective-permute-start.8 = (bf16[128,2560]{1,0:T(8,128)(2,1)S(1)}, bf16[128,2560]{1,0:T(8,128)(2,1)S(1)}, u32[]{:S(2)}, u32[]{:S(2)}) collective-permute-start(bf16[128,2560]{1,0:T(8,128)(2,1)S(1)} %part_of.7), channel_id=1, source_target_pairs={{0,2},{1,3},{2,4},{3,5},{4,6},{5,7},{6,0},{7,1},{8,10},{9,11},{10,... | collective-permute-start | bytes 1966088 | tf_op jit(solution)/shard_map/ppermute | solution.py:541
  34.0 36.5 %collective-permute-start.3 = (bf16[128,4096]{1,0:T(8,128)(2,1)S(1)}, bf16[128,4096]{1,0:T(8,128)(2,1)S(1)}, u32[]{:S(2)}, u32[]{:S(2)}) collective-permute-start(bf16[128,4096]{1,0:T(8,128)(2,1)S(1)} %part_of.4), channel_id=1, source_target_pairs={{0,1},{1,0},{2,3},{3,2},{4,5},{5,4},{6,7},{7,6},{8,9},{9,8},{10,11... | collective-permute-start | bytes 3145736 | tf_op jit(solution)/shard_map/ppermute | solution.py:546
  44.5 29.3 %collective-permute-start.6 = (bf16[128,4096]{1,0:T(8,128)(2,1)S(1)}, bf16[128,4096]{1,0:T(8,128)(2,1)S(1)}, u32[]{:S(2)}, u32[]{:S(2)}) collective-permute-start(bf16[128,4096]{1,0:T(8,128)(2,1)S(1)} %part_of.5), channel_id=1, source_target_pairs={{0,1},{1,0},{2,3},{3,2},{4,5},{5,4},{6,7},{7,6},{8,9},{9,8},{10,11... | collective-permute-start | bytes 3145736 | tf_op jit(solution)/shard_map/ppermute | solution.py:546
  59.2 13.3 %collective-permute-start.11 = (bf16[128,2560]{1,0:T(8,128)(2,1)S(1)}, bf16[128,2560]{1,0:T(8,128)(2,1)S(1)}, u32[]{:S(2)}, u32[]{:S(2)}) collective-permute-start(bf16[128,2560]{1,0:T(8,128)(2,1)S(1)} %collective-permute-done.10.refs_6_), channel_id=1, source_target_pairs={{0,1},{1,0},{2,3},{3,2},{4,5},{5,4},{6,7},{7,6},{8,9},{9,8},{10,11... | collective-permute-start | bytes 1966088 | tf_op jit(solution)/shard_map/ppermute | solution.py:546
  70.4 4.0 %collective-permute-start.9 = (bf16[128,2560]{1,0:T(8,128)(2,1)S(1)}, bf16[128,2560]{1,0:T(8,128)(2,1)S(1)}, u32[]{:S(2)}, u32[]{:S(2)}) collective-permute-start(bf16[128,2560]{1,0:T(8,128)(2,1)S(1)} %collective-permute-done.8.refs_4_), channel_id=1, source_target_pairs={{0,1},{1,0},{2,3},{3,2},{4,5},{5,4},{6,7},{7,6},{8,9},{9,8},{10,11... | collective-permute-start | bytes 1966088 | tf_op jit(solution)/shard_map/ppermute | solution.py:546
  70.4 13.4 %collective-permute-start.7 = (bf16[128,1536]{1,0:T(8,128)(2,1)S(1)}, bf16[128,1536]{1,0:T(8,128)(2,1)S(1)}, u32[]{:S(2)}, u32[]{:S(2)}) collective-permute-start(bf16[128,1536]{1,0:T(8,128)(2,1)S(1)} %part_of.6), channel_id=1, source_target_pairs={{0,2},{1,3},{2,4},{3,5},{4,6},{5,7},{6,0},{7,1},{8,10},{9,11},{10,... | collective-permute-start | bytes 1179656 | tf_op jit(solution)/shard_map/ppermute | solution.py:541
  70.5 10.7 %collective-permute-start.12 = (bf16[128,1024]{1,0:T(8,128)(2,1)S(1)}, bf16[128,1024]{1,0:T(8,128)(2,1)S(1)}, u32[]{:S(2)}, u32[]{:S(2)}) collective-permute-start(bf16[128,1024]{1,0:T(8,128)(2,1)S(1)} %get-tuple-element.46), channel_id=1, source_target_pairs={{8,0},{16,8},{24,16},{9,1},{17,9},{25,17},{10,2},{18,10},{26,18},{... | collective-permute-start | bytes 786440 | tf_op jit(solution)/shard_map/ppermute | solution.py:535
  72.5 8.7 %collective-permute-start = (s32[2,32]{1,0:T(2,128)S(1)}, s32[2,32]{1,0:T(2,128)S(1)}, u32[]{:S(2)}, u32[]{:S(2)}) collective-permute-start(s32[2,32]{1,0:T(2,128)S(1)} %pad_add_fusion.order_ref.refs_0_), channel_id=1, source_target_pairs={{8,0},{16,8},{24,16},{9,1},{17,9},{25,17},{10,2},{18,10},{26,18},{... | collective-permute-start | bytes 776 | tf_op jit(solution)/shard_map/ppermute | solution.py:535
  73.8 10.0 %collective-permute-start.14 = (bf16[128,1536]{1,0:T(8,128)(2,1)S(1)}, bf16[128,1536]{1,0:T(8,128)(2,1)S(1)}, u32[]{:S(2)}, u32[]{:S(2)}) collective-permute-start(bf16[128,1536]{1,0:T(8,128)(2,1)S(1)} %collective-permute-done.5.refs_0_.refs_8_.refs_6_), channel_id=1, source_target_pairs={{0,1},{1,0},{2,3},{3,2},{4,5},{5,4},{6,7},{7,6},{8,9},{9,8},{10,11... | collective-permute-start | bytes 1179656 | tf_op jit(solution)/shard_map/ppermute | solution.py:546
  89.9 10.2 %collective-permute-start.15 = (bf16[128,1024]{1,0:T(8,128)(2,1)S(1)}, bf16[128,1024]{1,0:T(8,128)(2,1)S(1)}, u32[]{:S(2)}, u32[]{:S(2)}) collective-permute-start(bf16[128,1024]{1,0:T(8,128)(2,1)S(1)} %attention.5), channel_id=1, source_target_pairs={{8,0},{16,8},{24,16},{9,1},{17,9},{25,17},{10,2},{18,10},{26,18},{... | collective-permute-start | bytes 786440 | tf_op jit(solution)/shard_map/ppermute | solution.py:535
  102.5 3.7 %collective-permute-start.18 = (bf16[128,1024]{1,0:T(8,128)(2,1)S(1)}, bf16[128,1024]{1,0:T(8,128)(2,1)S(1)}, u32[]{:S(2)}, u32[]{:S(2)}) collective-permute-start(bf16[128,1024]{1,0:T(8,128)(2,1)S(1)} %get-tuple-element.57), channel_id=1, source_target_pairs={{0,1},{1,0},{2,3},{3,2},{4,5},{5,4},{6,7},{7,6},{8,9},{9,8},{10,11... | collective-permute-start | bytes 786440 | tf_op jit(solution)/shard_map/ppermute | solution.py:546
  102.5 8.7 %collective-permute-start.16 = (bf16[96,1024]{1,0:T(8,128)(2,1)S(1)}, bf16[96,1024]{1,0:T(8,128)(2,1)S(1)}, u32[]{:S(2)}, u32[]{:S(2)}) collective-permute-start(bf16[96,1024]{1,0:T(8,128)(2,1)S(1)} %get-tuple-element.54), channel_id=1, source_target_pairs={{0,1},{1,2},{2,3},{3,4},{4,5},{5,6},{6,7},{8,9},{9,10},{10,11},{11... | collective-permute-start | bytes 589832 | tf_op jit(solution)/shard_map/ppermute | solution.py:535
  104.9 6.2 %collective-permute-start.17 = (bf16[96,1024]{1,0:T(8,128)(2,1)S(1)}, bf16[96,1024]{1,0:T(8,128)(2,1)S(1)}, u32[]{:S(2)}, u32[]{:S(2)}) collective-permute-start(bf16[96,1024]{1,0:T(8,128)(2,1)S(1)} %get-tuple-element.55), channel_id=1, source_target_pairs={{1,0},{2,1},{3,2},{4,3},{5,4},{6,5},{7,6},{9,8},{10,9},{11,10},{12... | collective-permute-start | bytes 589832 | tf_op jit(solution)/shard_map/ppermute | solution.py:535
  106.3 9.8 %collective-permute-start.19 = (bf16[32,1024]{1,0:T(8,128)(2,1)S(1)}, bf16[32,1024]{1,0:T(8,128)(2,1)S(1)}, u32[]{:S(2)}, u32[]{:S(2)}) collective-permute-start(bf16[32,1024]{1,0:T(8,128)(2,1)S(1)} %get-tuple-element.62), channel_id=1, source_target_pairs={{0,2},{1,3},{2,4},{3,5},{4,6},{5,7},{6,0},{7,1},{8,10},{9,11},{10,... | collective-permute-start | bytes 196616 | tf_op jit(solution)/shard_map/ppermute | solution.py:541
  108.6 7.5 %collective-permute-start.20 = (bf16[32,1024]{1,0:T(8,128)(2,1)S(1)}, bf16[32,1024]{1,0:T(8,128)(2,1)S(1)}, u32[]{:S(2)}, u32[]{:S(2)}) collective-permute-start(bf16[32,1024]{1,0:T(8,128)(2,1)S(1)} %get-tuple-element.63), channel_id=1, source_target_pairs={{0,4},{1,5},{2,6},{3,7},{4,0},{5,1},{6,2},{7,3},{8,12},{9,13},{10,... | collective-permute-start | bytes 196616 | tf_op jit(solution)/shard_map/ppermute | solution.py:541
  110.4 5.9 %collective-permute-start.21 = (bf16[32,1024]{1,0:T(8,128)(2,1)S(1)}, bf16[32,1024]{1,0:T(8,128)(2,1)S(1)}, u32[]{:S(2)}, u32[]{:S(2)}) collective-permute-start(bf16[32,1024]{1,0:T(8,128)(2,1)S(1)} %get-tuple-element.64), channel_id=1, source_target_pairs={{0,6},{1,7},{2,0},{3,1},{4,2},{5,3},{6,4},{7,5},{8,14},{9,15},{10,... | collective-permute-start | bytes 196616 | tf_op jit(solution)/shard_map/ppermute | solution.py:541
  116.4 9.5 %collective-permute-start.22 = (bf16[32,1024]{1,0:T(8,128)(2,1)S(1)}, bf16[32,1024]{1,0:T(8,128)(2,1)S(1)}, u32[]{:S(2)}, u32[]{:S(2)}) collective-permute-start(bf16[32,1024]{1,0:T(8,128)(2,1)S(1)} %chip_sum.1.refs_13_.refs_0_), channel_id=1, source_target_pairs={{0,2},{1,3},{2,4},{3,5},{4,6},{5,7},{6,0},{7,1},{8,10},{9,11},{10,... | collective-permute-start | bytes 196616 | tf_op jit(solution)/shard_map/ppermute | solution.py:541
  118.1 8.0 %collective-permute-start.23 = (bf16[32,1024]{1,0:T(8,128)(2,1)S(1)}, bf16[32,1024]{1,0:T(8,128)(2,1)S(1)}, u32[]{:S(2)}, u32[]{:S(2)}) collective-permute-start(bf16[32,1024]{1,0:T(8,128)(2,1)S(1)} %chip_sum.1.refs_13_.refs_0_), channel_id=1, source_target_pairs={{0,4},{1,5},{2,6},{3,7},{4,0},{5,1},{6,2},{7,3},{8,12},{9,13},{10,... | collective-permute-start | bytes 196616 | tf_op jit(solution)/shard_map/ppermute | solution.py:541
  118.9 7.1 %collective-permute-start.24 = (bf16[32,1024]{1,0:T(8,128)(2,1)S(1)}, bf16[32,1024]{1,0:T(8,128)(2,1)S(1)}, u32[]{:S(2)}, u32[]{:S(2)}) collective-permute-start(bf16[32,1024]{1,0:T(8,128)(2,1)S(1)} %chip_sum.1.refs_13_.refs_0_), channel_id=1, source_target_pairs={{0,6},{1,7},{2,0},{3,1},{4,2},{5,3},{6,4},{7,5},{8,14},{9,15},{10,... | collective-permute-start | bytes 196616 | tf_op jit(solution)/shard_map/ppermute | solution.py:541
  (21 other events, 161.6 us)
